TPU v7x, 128 devices: a whole 4x4x4 slice. The times are simulated.
128 devices in a mesh: freq: 4 (over z), grid: 32 (over y, x, core).
Axes of the slice: x: 4, y: 4, z: 4, core: 2. Of those that a mesh axis runs over, the one named last changes fastest.
Arguments:
- green_spectra: bfloat16 [2, 8, 2048, 8192], P(None, 'freq', None, 'grid'), may hold values from -6 to 6
- source_psd: float32 [8, 8192], P('freq', 'grid'), may hold values from 0.2 to 5
- pair_list: int32 [64, 2], replicated, may hold values from 0 to 15, as said below
- owner_map: int32 [64], replicated, may hold values from 0 to 31, as said below
- observed: bfloat16 [64, 128, 128, 128], P('grid'), may hold values from -48 to 48
Outputs:
- gradient: float32 [8, 8192], P('freq', 'grid')
- misfit: float32 [64, 128], P('grid', 'freq')
Inputs may be any that keep to these rules, and one draw needn't show every extreme that they name: `pair_list`: each row names two different station blocks, the smaller first; no pair of blocks is listed twice. `owner_map`: each owner appears exactly 2 times.
All inputs are finite; a program needn't handle non-finite values.
Results may differ from a plain program's by a relative error of at most 0.0014.
Values may be sent and summed in bfloat16 or wider, within the bound.
A program may use at most 128 MiB of HBM per device.

v0:
```python
import math

import jax
import jax.numpy as jnp
from jax import lax
from jax.sharding import PartitionSpec as P

harmonic_step = 3


def phase_values(freq_total, lag_count):
    freq_ids = jnp.arange(freq_total, dtype=jnp.int32)[:, None]
    lag_ids = jnp.arange(lag_count, dtype=jnp.int32)[None, :]
    turns = (harmonic_step * (freq_ids + 1) * lag_ids % lag_count).astype(jnp.float32)
    angles = turns * jnp.float32(2.0 * math.pi / lag_count)
    return jnp.stack((jnp.cos(angles), -jnp.sin(angles)))


def local(green_spectra, source_psd, pair_list, owner_map, observed):
    highest = lax.Precision.HIGHEST
    grid_devices = lax.axis_size("grid")
    freq_devices = lax.axis_size("freq")
    planes, freq_dev, stations, points = green_spectra.shape
    pair_dev, block_size, unused_cols, lag_count = observed.shape
    slot_count = owner_map.shape[0]
    block_count = stations // block_size
    freq_total = freq_dev * freq_devices
    root_scale = 1.0 / math.sqrt(points * grid_devices)
    slot_order = jnp.argsort(owner_map, stable=True)
    first_blocks = jnp.take(pair_list[:, 0], slot_order)
    second_blocks = jnp.take(pair_list[:, 1], slot_order)
    weighted = (green_spectra * source_psd[None, :, None, :]).astype(jnp.bfloat16)
    weighted_blocks = weighted.reshape(planes, freq_dev, block_count, block_size, points)
    plain_blocks = green_spectra.reshape(planes, freq_dev, block_count, block_size, points)
    group_size = math.gcd(slot_count, 8)
    left_ids = first_blocks.reshape(slot_count // group_size, group_size)
    right_ids = second_blocks.reshape(slot_count // group_size, group_size)

    def one_group(block_ids):
        left_block = jnp.take(weighted_blocks, block_ids[0], axis=2)
        right_block = jnp.take(plain_blocks, block_ids[1], axis=2)
        turned = jnp.stack((-right_block[1], right_block[0]))
        real_part = jnp.einsum(
            "cfsix,cfsjx->sfij", left_block, right_block, preferred_element_type=jnp.float32
        )
        imag_part = jnp.einsum(
            "cfsix,cfsjx->sfij", left_block, turned, preferred_element_type=jnp.float32
        )
        return jnp.stack((real_part, imag_part), axis=1) * jnp.float32(root_scale)

    grouped = lax.map(one_group, (left_ids, right_ids))
    totals = lax.psum(
        grouped.reshape(slot_count, 2, freq_dev, block_size, block_size).astype(jnp.bfloat16),
        "grid",
    ).astype(jnp.float32)
    owned = lax.dynamic_slice_in_dim(totals, lax.axis_index("grid") * pair_dev, pair_dev, 0)
    phases = phase_values(freq_total, lag_count)
    quarter_rows = block_size // freq_devices
    freq_index = lax.axis_index("freq")
    quarter = lax.all_to_all(owned, "freq", split_axis=3, concat_axis=2, tiled=True)
    observed_rows = lax.dynamic_slice_in_dim(
        observed, freq_index * quarter_rows, quarter_rows, 1
    ).astype(jnp.float32)
    modelled = jnp.einsum("skfij,kft->sijt", quarter, phases, precision=highest)
    residual = modelled - observed_rows
    misfit = jnp.sum(residual * residual, axis=(2, 3)) / jnp.float32(
        2.0 * block_size * lag_count * freq_total
    )
    adjoint_rows = (
        jnp.einsum("sijt,kft->skfij", residual, phases, precision=highest) / jnp.float32(lag_count)
    ).astype(jnp.bfloat16)
    adjoint = lax.all_to_all(adjoint_rows, "freq", split_axis=2, concat_axis=3, tiled=True)
    shard_piece = lax.all_gather(adjoint, "grid", axis=0, tiled=True)
    length = shard_piece.shape[0]
    group_size = math.gcd(length, 8)
    left_ids = first_blocks
    right_ids = second_blocks

    def add_group(group_index, partial_sum):
        offset = group_index * group_size
        left_block = jnp.take(
            plain_blocks, lax.dynamic_slice_in_dim(left_ids, offset, group_size), axis=2
        )
        right_block = jnp.take(
            plain_blocks, lax.dynamic_slice_in_dim(right_ids, offset, group_size), axis=2
        )
        weights = lax.dynamic_slice_in_dim(shard_piece, offset, group_size, 0)
        along_term = jnp.einsum(
            "skfij,kfsjx->sfix",
            weights,
            jnp.stack((right_block[0], -right_block[1])),
            preferred_element_type=jnp.float32,
        )
        across_term = jnp.einsum(
            "skfij,kfsjx->sfix",
            weights,
            jnp.stack((right_block[1], right_block[0])),
            preferred_element_type=jnp.float32,
        )
        real_side = jnp.einsum(
            "fsix,sfix->fx",
            left_block[0],
            along_term,
            precision=highest,
            preferred_element_type=jnp.float32,
        )
        imag_side = jnp.einsum(
            "fsix,sfix->fx",
            left_block[1],
            across_term,
            precision=highest,
            preferred_element_type=jnp.float32,
        )
        return partial_sum + real_side + imag_side

    summed = lax.fori_loop(
        0, length // group_size, add_group, jnp.zeros((freq_dev, points), jnp.float32)
    )
    gradient = summed * jnp.float32(1.0 / (block_size * math.sqrt(slot_count)))
    return (gradient, misfit)


def solution(mesh):
    in_specs = (
        P(None, "freq", None, "grid"),
        P("freq", "grid"),
        P(),
        P(),
        P("grid", None, None, None),
    )
    out_specs = (P("freq", "grid"), P("grid", "freq"))
    return jax.shard_map(local, mesh=mesh, in_specs=in_specs, out_specs=out_specs, check_vma=False)
```

profile of v0, /device:TPU:1, one launch (start us, length us, event | category | flops | bytes accessed | tf_op | source)
XLA Modules:
  0.0 475.6 jit_solution(17062320096147027596)
XLA Ops:
  7.2 2.7 sort.17
  12.4 4.9 %multiply_convert_fusion = bf16[2,2,2048,256]{3,2,1,0:T(8,128)(2,1)} fusion(bf16[2,2,2048,256]{3,2,1,0:T(8,128)(2,1)} %param.13, f32[2,256]{1,0:T(2,128)} %param.14), kind=kLoop, calls=%fused_computation.63 | loop fusion | flops 6291456 | bytes 8390656 | tf_op jit(solution)/shard_map/convert_element_type | solution.py:32
  17.3 130.1 %while.24 = (s32[]{:T(128)}, bf16[8,8,2,2,128,128]{5,4,3,2,1,0:T(8,128)(2,1)}, s32[8,8]{1,0:T(8,128)S(1)}, bf16[2,2,16,128,256]{4,3,2,1,0:T(8,128)(2,1)}, s32[8,...) while((s32[]{:T(128)}, bf16[8,8,2,2,128,128]{5,4,3,2,1,0:T(8,128)(2,1)}, ...), condition=%wide.region_2.5_spmd, body=%wide.region_1.0_spmd.sunk | while | flops 543164544 | bytes 38806420 | solution.py:51
  17.4 4.2 gather_fusion
  21.6 1.9 fusion.85
  24.6 4.2 gather_fusion.1
  28.8 2.8 fusion.86
  33.6 4.2 gather_fusion
  37.8 1.9 fusion.85
  40.8 4.2 gather_fusion.1
  45.0 2.8 fusion.86
  49.9 4.2 gather_fusion
  54.1 1.9 fusion.85
  57.1 4.2 gather_fusion.1
  61.3 2.8 fusion.86
  66.2 4.2 gather_fusion
  70.4 1.9 fusion.85
  73.4 4.2 gather_fusion.1
  77.6 2.7 fusion.86
  82.4 4.2 gather_fusion
  86.7 1.9 fusion.85
  89.6 4.2 gather_fusion.1
  93.8 2.7 fusion.86
  98.7 4.2 gather_fusion
  102.9 1.9 fusion.85
  105.9 4.2 gather_fusion.1
  110.1 2.7 fusion.86
  115.0 4.2 gather_fusion
  119.2 1.9 fusion.85
  122.2 4.2 gather_fusion.1
  126.4 2.7 fusion.86
  131.2 4.2 gather_fusion
  135.4 1.9 fusion.85
  138.4 4.2 gather_fusion.1
  142.6 2.7 fusion.86
  147.5 123.7 %all-reduce.2.cloned.1.call-done = bf16[64,2,2,128,128]{4,3,2,1,0:T(8,128)(2,1)} async-done(((bf16[64,2,2,128,128]{4,3,2,1,0:T(8,128)(2,1)}), bf16[64,2,2,128,128]{4,3,2,1,0:T(8,128)(2,1)}) %all-reduce.2.cloned.1.call-update) | async-done | bytes 8388624 | tf_op jit(solution)/shard_map/psum | solution.py:52
  273.4 4.1 all-to-all-start
  277.6 7.9 %all-to-all-done = f32[2,2,2,128,128]{4,2,1,0,3:T(2,128)S(1)} async-done(((f32[2,2,2,128,128]{4,2,1,0,3:T(2,128)}), f32[2,2,2,128,128]{4,2,1,0,3:T(2,128)S(1)}, u32[]{:S(2)}, u32[]{:S(2)}) %all-to-all-start) | async-done | bytes 524320 | tf_op jit(solution)/shard_map/all_to_all | solution.py:60
  286.1 9.8 %multiply_reduce_fusion = (f32[2,32]{1,0:T(2,128)S(1)}, f32[2,32,128,128,1]{3,2,4,1,0:T(8,128)S(1)}) fusion(bf16[2,128,128,128]{3,2,1,0:T(8,128)(2,1)} %param.17, s32[]{:T(128)S(6)} %select_n.51, f32[2,2,8,32,128]{4,2,1,3,0:T(8,128)S(1)} %bitcast.138, f32[1,8,128]{2,1,0:T(8,128)S(1)} %get-tuple-element.226, f32[1,8,128]{2,1,0:T(8,128)S(1)} %get-tuple-element.225), kind=kOutput, calls=%fused_computation.67 | convolution fusion | flops 205522880 | bytes 6824196 | tf_op jit(solution)/shard_map/skfij,kft->sijt/dot_general | solution.py:64
  295.9 5.1 %fusion.48 = bf16[2,2,8,32,128]{4,2,3,0,1:T(8,128)(2,1)S(1)} fusion(f32[2,32,128,128,1]{3,2,4,1,0:T(8,128)S(1)} %get-tuple-element.230, bf16[2,128,128,128]{3,2,1,0:T(8,128)(2,1)} %param.17, s32[]{:T(128)S(6)} %select_n.51, f32[1,8,128]{2,1,0:T(8,128)S(1)} %get-tuple-element.226, f32[1,8,128]{2,1,0:T(8,128)S(1)} %get-tuple-element.225), kind=kOutput, calls=%fused_computation.71 | convolution fusion | flops 203687936 | bytes 6561796 | tf_op jit(solution)/shard_map/sijt,kft->skfij/dot_general | solution.py:70
  301.0 7.9 %all_to_all.36 = bf16[2,2,8,32,128]{4,3,0,1,2:T(8,128)(2,1)S(1)} all-to-all(bf16[2,2,8,32,128]{4,3,0,1,2:T(8,128)(2,1)S(1)} %copy.34), channel_id=1, replica_groups=mesh['freq'=4,'grid'=32] {'freq'}, dimensions={2} | all-to-all | bytes 524288 | tf_op jit(solution)/shard_map/all_to_all | solution.py:72
  310.3 54.4 %all-gather.2.cloned.1.call-done = bf16[64,2,2,128,128]{4,3,2,1,0:T(8,128)(2,1)} async-done(((bf16[2,2,2,128,128]{4,3,2,1,0:T(8,128)(2,1)}), bf16[64,2,2,128,128]{4,3,2,1,0:T(8,128)(2,1)}) %all-gather.2.cloned.1.call-update) | async-done | bytes 8388624 | tf_op jit(solution)/shard_map/all_gather | solution.py:73
  364.6 103.5 %while.25 = (s32[]{:T(128)}, f32[2,256]{1,0:T(2,128)S(1)}, s32[64]{0:T(128)S(1)}, bf16[2,2,16,128,256]{4,3,2,1,0:T(8,128)(2,1)}, bf16[64,2,2,128,128]{4,3,2,1,0:...) while((s32[]{:T(128)}, f32[2,256]{1,0:T(2,128)S(1)}, ...), condition=%wide.region_5.8_spmd.clone, body=%wide.region_4.7_spmd.clone.sunk | while | flops 544737920 | bytes 38818300 | solution.py:116
  364.7 2.9 gather_fusion.2
  369.5 2.9 gather_fusion.3
  377.7 2.9 gather_fusion.2
  382.4 2.9 gather_fusion.3
  388.6 1.8 fusion.93
  390.6 2.9 gather_fusion.2
  395.3 2.9 gather_fusion.3
  401.6 1.8 fusion.93
  403.5 2.9 gather_fusion.2
  408.3 2.9 gather_fusion.3
  414.5 1.8 fusion.93
  416.5 2.9 gather_fusion.2
  421.2 2.9 gather_fusion.3
  429.4 2.9 gather_fusion.2
  434.2 2.9 gather_fusion.3
  440.4 1.8 fusion.93
  442.4 2.9 gather_fusion.2
  447.1 2.9 gather_fusion.3
  453.3 1.8 fusion.93
  455.3 2.9 gather_fusion.2
  460.1 2.9 gather_fusion.3
  (188 shorter events, 80.8 us)
Async XLA Ops:
  7.2 264.0 %all-reduce.2.cloned.1.call-start = ((), (), s32[]{:S(2)}) async-start(), calls=%async_computation.2 | async-start | bytes 16777216 | tf_op jit(solution)/shard_map/psum | solution.py:52
  28.8 2.8 copy-start
  45.0 2.8 copy-start
  61.3 2.8 copy-start
  77.6 2.8 copy-start
  93.8 2.8 copy-start
  110.1 2.8 copy-start
  126.4 2.8 copy-start
  142.6 2.8 copy-start
  273.4 12.2 %all-to-all-start = ((f32[2,2,2,128,128]{4,2,1,0,3:T(2,128)}), f32[2,2,2,128,128]{4,2,1,0,3:T(2,128)S(1)}, u32[]{:S(2)}, u32[]{:S(2)}) async-start(f32[2,2,2,128,128]{4,2,1,0,3:T(2,128)} %copy.31), calls=%async_computation | async-start | bytes 1048576 | tf_op jit(solution)/shard_map/all_to_all | solution.py:60
  277.5 87.1 %all-gather.2.cloned.1.call-start = ((), (), s32[]{:S(2)}) async-start(), calls=%async_computation.3 | async-start | bytes 8650752 | tf_op jit(solution)/shard_map/all_gather | solution.py:73
  372.3 1.2 copy-start.1
  372.3 1.5 copy-start.2
  385.3 1.2 copy-start.1
  385.3 1.5 copy-start.2
  398.2 1.2 copy-start.1
  398.2 1.5 copy-start.2
  411.2 1.2 copy-start.1
  411.2 1.5 copy-start.2
  424.1 1.2 copy-start.1
  424.1 1.5 copy-start.2
  437.0 1.2 copy-start.1
  437.0 1.5 copy-start.2
  450.0 1.2 copy-start.1
  450.0 1.5 copy-start.2
  462.9 1.2 copy-start.1
  462.9 1.5 copy-start.2
Sparse Core Ops, SparseCore 0:
  147.6 123.5 all-reduce.1
  309.8 54.7 all-gather.1
where the time goes:
time: 478 us; the launch traced here: 476 us
  waiting for transfers between devices  186 us (39%)
  local copies, waits for them, and re-layouts  128 us (27%)
  matrix products  72.1 us (15%)
  other arithmetic  62.1 us (13%)
  between operations  14.1 us (3%)
  blocking collectives  7.92 us (2%)
    psum x1, waiting for transfers between devices, local(): lax.psum(grouped.reshape(slot_count, 2, freq_dev, block_size, block_size)...  124 us
    all_gather x1, waiting for transfers between devices, local(): shard_piece = lax.all_gather(adjoint, 'grid', axis=0, tiled=True)  54.4 us
    gather x8, local copies, waits for them, and re-layouts, one_group(): right_block = jnp.take(plain_blocks, block_ids[1], axis=2)  33.7 us
    gather x8, local copies, waits for them, and re-layouts, one_group(): left_block = jnp.take(weighted_blocks, block_ids[0], axis=2)  33.6 us
    gather x8, local copies, waits for them, and re-layouts, add_group(): jnp.take(plain_blocks, lax.dynamic_slice_in_dim(right_ids, offset, group_...  23 us
    gather x8, local copies, waits for them, and re-layouts, add_group(): jnp.take(plain_blocks, lax.dynamic_slice_in_dim(left_ids, offset, group_s...  22.9 us
    dot_general x8, matrix products, one_group(): jnp.einsum('cfsix,cfsjx->sfij', left_block, turned, preferred_element_typ...  22 us
    select_n x8, other arithmetic, one_group(): right_block = jnp.take(plain_blocks, block_ids[1], axis=2)  14.8 us
  transfers between devices with their start and end apart: 3, of which 3 were waited for; matrix products, arithmetic and copies ran while one was open for 0% of the time, Pallas kernels for 0%

commit v1 on v0

v1 whole, which is shorter than its diff:
```python
import functools
import math

import jax
import jax.numpy as jnp
import ml_dtypes
import numpy as np
from jax import lax
from jax.experimental import pallas as pl
from jax.experimental.pallas import tpu as pltpu
from jax.sharding import PartitionSpec as P

harmonic_step = 3
side = 4
stages = 2
pieces = 3
group = 8
MESH = pl.DeviceIdType.MESH
f32 = jnp.float32
bf16 = jnp.bfloat16


def phase_table(freq_total, lag_count, freq_devices):
    freq_ids = np.arange(freq_total)[:, None]
    turns = harmonic_step * (freq_ids + 1) * np.arange(lag_count)[None, :] % lag_count
    angles = turns * (2.0 * math.pi / lag_count)
    exact = np.stack((np.cos(angles), -np.sin(angles)), axis=1)
    parts = []
    for unused in range(pieces):
        part = exact.astype(ml_dtypes.bfloat16)
        parts.append(part)
        exact = exact - part.astype(np.float64)
    table = np.stack(parts).reshape(pieces, freq_devices, 2, 2, lag_count)
    both = np.stack((table, table[:, :, ::-1]), axis=2)
    both = both.transpose(1, 2, 0, 3, 4, 5).reshape(freq_devices * 2, pieces * 4, lag_count)
    return np.repeat(both, group, axis=1)


def kernel(
    freq_devices,
    ids,
    psd,
    table,
    green,
    observed,
    gradient_out,
    misfit_out,
    gbuf,
    wbuf,
    psd_other,
    obs,
    phi,
    spread,
    ohat,
    ohat_send,
    energy,
    send1,
    recv1,
    send_a,
    recv_a,
    send_b,
    recv_b,
    keep,
    abuf,
    total,
    mis_own,
    mis_other,
    mis_pair,
    mis_freq,
    gsum,
    gsend,
    grecv,
    local_sem,
    core_send,
    core_recv,
    one_send,
    one_recv,
    a_send,
    a_recv,
    b_send,
    b_recv,
    g1_send,
    g1_recv,
    g1f_send,
    g1f_recv,
    g2_send,
    g2_recv,
    g2f_send,
    g2f_recv,
    z_send,
    z_recv,
):
    z = lax.axis_index("freq")
    g = lax.axis_index("grid")
    c = g % 2
    x = (g // 2) % side
    y = g // (2 * side)
    other = g + 1 - 2 * c
    points = psd.shape[1]
    pair_dev, block, unused_cols, lags = observed.shape
    freq_total = 2 * freq_devices
    slot_count = 2 * side * side * pair_dev
    root_scale = 1.0 / math.sqrt(points * 2 * side * side)

    def neighbour(axis, d):
        step = 1 + 2 * d
        nx = (x + (1 - axis) * step) % side
        ny = (y + axis * step) % side
        return (ny * side + nx) * 2 + c

    def slot_of(t, h, o, r):
        sx = (x + (1 - h) * o + h * r) % side
        sy = (y + h * o + (1 - h) * r) % side
        return (sy * side + sx) * 4 + h * 2 + t

    def lane(d, j):
        return (1 - d) * (2 - 2 * j) + d * (1 + 2 * j)

    def lane_place(r):
        return ((r + 1) // 2 + 1) % 2

    def remote(src, dst, send, recv, device):
        return pltpu.make_async_remote_copy(
            src_ref=src, dst_ref=dst, send_sem=send, recv_sem=recv,
            device_id={"grid": device}, device_id_type=MESH,
        )

    own_points = pl.ds(0, points)
    other_points = pl.ds(points, points)
    load_green = [
        pltpu.make_async_copy(green.at[k, c], gbuf.at[k, :, :, own_points], local_sem.at[k])
        for k in range(2)
    ]
    load_table = pltpu.make_async_copy(table.at[z * 2 + c], phi, local_sem.at[2])
    load_obs = pltpu.make_async_copy(observed, obs, local_sem.at[3])
    for copy in load_green:
        copy.start()
    load_table.start()
    load_obs.start()

    barrier = pltpu.get_barrier_semaphore()
    friends = [{"grid": other}]
    for axis in range(2):
        for d in range(2):
            friends.append({"grid": neighbour(axis, d)})
    for dz in range(1, freq_devices):
        friends.append({"freq": (z + dz) % freq_devices})
    for friend in friends:
        pl.semaphore_signal(barrier, inc=1, device_id=friend, device_id_type=MESH)
    pl.semaphore_wait(barrier, len(friends))

    swap_psd = remote(psd, psd_other, core_send.at[2], core_recv.at[2], other)
    swap_green = [
        remote(
            green.at[k, 1 - c], gbuf.at[k, :, :, other_points], core_send.at[k], core_recv.at[k], other
        )
        for k in range(2)
    ]
    swap_psd.start()
    for copy in swap_green:
        copy.start()

    def weigh(k, where, row):
        def body(b, carry):
            wbuf[k, b, :, where] = (gbuf[k, b, :, where].astype(f32) * row).astype(bf16)
            return carry

        lax.fori_loop(0, gbuf.shape[1], body, 0)

    own_row = psd[pl.ds(c, 1), :]
    for k in range(2):
        load_green[k].wait()
        weigh(k, own_points, own_row)
    swap_psd.wait_recv()
    other_row = psd_other[pl.ds(c, 1), :]
    for k in range(2):
        swap_green[k].wait_recv()
        weigh(k, other_points, other_row)

    load_table.wait()
    rows = phi.shape[0]
    row_in_group = lax.broadcasted_iota(jnp.int32, (rows, lags), 0) % group
    phi_values = phi[...].astype(f32)
    for i in range(group):
        spread[:, pl.ds(i * lags, lags)] = jnp.where(row_in_group == i, phi_values, 0.0).astype(bf16)

    def unit(slot):
        left = wbuf[:, ids[slot]].reshape(2 * block, 2 * points)
        right = gbuf[:, ids[slot_count + slot]].reshape(2 * block, 2 * points)
        acc = lax.dot_general(left, right, (((1,), (1,)), ((), ())), preferred_element_type=f32)
        real = acc[:block, :block] + acc[block:, block:]
        imag = acc[block:, :block] - acc[:block, block:]
        return real, imag

    def copy1(n):
        u = n % 8
        return remote(
            send1.at[n], recv1.at[n], one_send.at[n], one_recv.at[n], neighbour(u % 2, (u // 2) % 2)
        )

    def first_ring(low, high):
        def body(n, carry):
            t = n // 24
            role = (n % 24) // 8
            u = n % 8
            h, d, j = u % 2, (u // 2) % 2, u // 4
            near = 1 + 2 * d
            o = jnp.where(role == 0, 2, near)
            r = jnp.where(role == 1, lane(1 - d, j), lane(d, j))
            real, imag = unit(slot_of(t, h, o, r))

            @pl.when(role == 2)
            def _():
                copy1(n - 16).wait_recv()
                send1[n, 0] = (real + recv1[n - 16, 0].astype(f32)).astype(bf16)
                send1[n, 1] = (imag + recv1[n - 16, 1].astype(f32)).astype(bf16)

            @pl.when(role != 2)
            def _():
                send1[n, 0] = real.astype(bf16)
                send1[n, 1] = imag.astype(bf16)

            copy1(n).start()
            return carry

        lax.fori_loop(low, high, body, 0)

    def arrival1(t, h, d, r):
        role = 2 - (r + d) % 2
        return t * 24 + role * 8 + lane_place(r) * 4 + d * 2 + h

    def line_sum(t, h, r):
        real, imag = unit(slot_of(t, h, 0, r))
        for d in range(2):
            n = arrival1(t, h, d, r)
            copy1(n).wait_recv()
            real = real + recv1[n, 0].astype(f32)
            imag = imag + recv1[n, 1].astype(f32)
        return real, imag

    def place(t, h, d):
        return (t * 2 + h) * 2 + d

    def copy_a(t, h, d):
        i = place(t, h, d)
        return remote(send_a.at[i], recv_a.at[i], a_send.at[i], a_recv.at[i], neighbour(1 - h, d))

    def copy_b(t, h, d, k):
        i = place(t, h, d)
        return remote(
            send_b.at[i, k], recv_b.at[i, k], b_send.at[i * 2 + k], b_recv.at[i * 2 + k],
            neighbour(1 - h, d),
        )

    def second_ring_open(t):
        def body(v, carry):
            h, w = v % 2, v // 2
            r = jnp.where(w == 0, 2, 2 * w - 1)
            real, imag = line_sum(t, h, r)

            @pl.when(w == 0)
            def _():
                send_a[place(t, h, 0)] = real.astype(bf16)
                copy_a(t, h, 0).start()
                send_a[place(t, h, 1)] = imag.astype(bf16)
                copy_a(t, h, 1).start()

            @pl.when(w == 1)
            def _():
                i = place(t, h, 0)
                send_b[i, 1] = imag.astype(bf16)
                keep[i] = real
                copy_b(t, h, 0, 1).start()

            @pl.when(w == 2)
            def _():
                i = place(t, h, 1)
                send_b[i, 0] = real.astype(bf16)
                keep[i] = imag
                copy_b(t, h, 1, 0).start()

            return carry

        lax.fori_loop(0, 6, body, 0)

    def second_ring_close(t):
        def body(v, carry):
            h, d = v % 2, v // 2
            i = place(t, h, d)
            copy_a(t, h, d).wait_recv()
            send_b[i, d] = (keep[i] + recv_a[i].astype(f32)).astype(bf16)
            copy_b(t, h, d, d).start()
            return carry

        lax.fori_loop(0, 4, body, 0)

    def copy_g1(t, h, d):
        s, i = slot_of(t, h, 0, 0), place(t, h, d)
        return remote(abuf.at[s], abuf.at[s], g1_send.at[i], g1_recv.at[i], neighbour(1 - h, d))

    def copy_g1f(t, h, d):
        s, i = slot_of(t, h, 0, 3 - 2 * d), place(t, h, d)
        return remote(abuf.at[s, d], abuf.at[s, d], g1f_send.at[i], g1f_recv.at[i], neighbour(1 - h, d))

    def copy_g2(t, h, d, r):
        s, i = slot_of(t, h, 0, r), place(t, h, d) * 4 + r
        return remote(abuf.at[s], abuf.at[s], g2_send.at[i], g2_recv.at[i], neighbour(h, d))

    def copy_g2f(t, h, d, j):
        s, i = slot_of(t, h, 3 - 2 * d, lane(d, j)), place(t, h, d) * 2 + j
        return remote(abuf.at[s], abuf.at[s], g2f_send.at[i], g2f_recv.at[i], neighbour(h, d))

    ones = jnp.ones((8, block), f32)

    def lane_sum(values):
        return lax.dot_general(
            ones[:, : values.shape[1]], values, (((1,), (1,)), ((), ())),
            precision=lax.Precision.HIGHEST, preferred_element_type=f32,
        )

    def own_adjoint(t):
        def body(h, carry):
            real, imag = line_sum(t, h, 0)
            for d in range(2):
                i = place(t, h, d)
                for k in range(2):
                    copy_b(t, h, d, k).wait_recv()
                real = real + recv_b[i, 0].astype(f32)
                imag = imag + recv_b[i, 1].astype(f32)
            s = slot_of(t, h, 0, 0)
            q = h * 2 + t
            kept = jnp.zeros_like(real)
            for k, value in enumerate((real, imag)):
                cross = value * f32(root_scale)
                seen = ohat[q, k]
                abuf[s, k] = (0.5 * cross - seen * f32(1.0 / lags)).astype(bf16)
                kept = kept + cross * (f32(lags / 2) * cross - 2.0 * seen)
            for d in range(2):
                copy_g1(t, h, d).start()
            for d in range(2):
                copy_g2(t, h, d, 0).start()
            total[q] = kept
            return carry

        lax.fori_loop(0, 2, body, 0)

    def gather_1(t):
        def body(v, carry):
            h, d = v % 2, v // 2
            copy_g1(t, h, d).wait_recv()
            copy_g1f(t, h, d).start()
            for side_d in range(2):
                copy_g2(t, h, side_d, 3 - 2 * d).start()
            return carry

        lax.fori_loop(0, 4, body, 0)

    def gather_2(t):
        def body(h, carry):
            for d in range(2):
                copy_g1f(t, h, d).wait_recv()
            for d in range(2):
                copy_g2(t, h, d, 2).start()
            return carry

        lax.fori_loop(0, 2, body, 0)

    def gather_lane(t, r):
        e = r % 2
        j = lane_place(r)

        def body(h, carry):
            copy_g2(t, h, e, r).wait_recv()
            copy_g2f(t, h, e, j).start()
            copy_g2(t, h, 1 - e, r).wait_recv()
            return carry

        lax.fori_loop(0, 2, body, 0)

    def gather_end(t, r):
        def body(h, carry):
            copy_g2f(t, h, r % 2, lane_place(r)).wait_recv()
            return carry

        lax.fori_loop(0, 2, body, 0)

    def back(t, count, choose):
        def body(v, carry):
            h, w = v % 2, v // 2
            o, r = choose(w)
            s = slot_of(t, h, o, r)
            weights = abuf[s]
            top = jnp.concatenate((weights[0], -weights[1]), axis=1)
            low = jnp.concatenate((weights[1], weights[0]), axis=1)
            right = gbuf[:, ids[slot_count + s]].reshape(2 * block, 2 * points)
            moved = jnp.dot(
                jnp.concatenate((top, low), axis=0), right, preferred_element_type=f32
            )
            left = gbuf[:, ids[s]].reshape(2 * block, 2 * points).astype(f32)
            return carry + jnp.sum((moved * left).reshape(2 * block // 8, 8, 2 * points), axis=0)

        gsum[...] = lax.fori_loop(0, 2 * count, body, gsum[...])

    def project():
        load_obs.wait()

        def body(i, carry):
            first = pl.multiple_of(i * group, group)
            seen = jnp.concatenate(
                [
                    jnp.concatenate([obs[s, first + k] for k in range(group)], axis=1)
                    for s in range(pair_dev)
                ],
                axis=0,
            )
            out = lax.dot_general(
                spread[...], seen, (((1,), (1,)), ((), ())), preferred_element_type=f32
            )
            out = jnp.sum(out.reshape(pieces, 4 * group, pair_dev * block), axis=0)
            for s in range(pair_dev):
                for k in range(2):
                    cols = slice(s * block, (s + 1) * block)
                    ohat[2 * c + s, k, pl.ds(first, group), :] = out[k * group : (k + 1) * group, cols]
                    ohat_send[s, k, pl.ds(first, group), :] = out[(2 + k) * group : (3 + k) * group, cols]
            return carry

        lax.fori_loop(0, block // group, body, 0)

    swap_ohat = remote(
        ohat_send, ohat.at[pl.ds(2 * c, 2)], core_send.at[3], core_recv.at[3], other
    )
    part_rows = block // freq_devices

    def energies():
        def body(i, carry):
            for s in range(pair_dev):
                seen = obs[s, z * part_rows + i].astype(f32)
                energy[pl.ds(s * part_rows + i, 1), :] = jnp.sum(seen * seen, axis=0, keepdims=True)
            return carry

        lax.fori_loop(0, part_rows, body, 0)

    gsum[...] = jnp.zeros_like(gsum)
    first_ring(0, 40)
    second_ring_open(0)
    project()
    swap_ohat.start()
    first_ring(40, 48)
    second_ring_close(0)
    swap_ohat.wait_recv()
    own_adjoint(0)
    second_ring_open(1)
    gather_1(0)
    second_ring_close(1)
    own_adjoint(1)
    gather_2(0)
    back(0, 1, lambda w: (0, 0))
    gather_lane(0, 0)
    gather_1(1)
    back(1, 1, lambda w: (0, 0))
    back(0, 2, lambda w: (1 + 2 * w, 0))
    gather_2(1)
    gather_lane(1, 0)
    back(0, 3, lambda w: (0, 1 + w))
    energies()
    gather_lane(0, 1)
    gather_lane(0, 3)
    back(1, 2, lambda w: (1 + 2 * w, 0))
    back(1, 3, lambda w: (0, 1 + w))

    mis_own[...] = jnp.zeros_like(mis_own)
    for q in range(2 * stages):
        mis_own[pl.ds(q, 1), :] = lane_sum(total[q])[:1]
    swap_mis = remote(mis_own, mis_other, core_send.at[4], core_recv.at[4], other)
    swap_mis.start()

    back(0, 4, lambda w: (1 + 2 * (w % 2), 1 + 2 * (w // 2)))
    gather_lane(0, 2)
    gather_lane(1, 1)
    gather_lane(1, 3)
    swap_mis.wait_recv()
    mis_pair[...] = mis_own[...] + mis_other[...]

    def copy_z(dz):
        return pltpu.make_async_remote_copy(
            src_ref=mis_pair, dst_ref=mis_freq.at[dz - 1],
            send_sem=z_send.at[dz - 1], recv_sem=z_recv.at[dz - 1],
            device_id={"freq": (z + dz) % freq_devices}, device_id_type=MESH,
        )

    for dz in range(1, freq_devices):
        copy_z(dz).start()
    back(0, 2, lambda w: (1 + 2 * w, 2))
    back(1, 4, lambda w: (1 + 2 * (w % 2), 1 + 2 * (w // 2)))
    gather_lane(1, 2)
    back(1, 2, lambda w: (1 + 2 * w, 2))

    mine = mis_pair[...]
    for dz in range(1, freq_devices):
        copy_z(dz).wait_recv()
        mine = mine + mis_freq[dz - 1]
    mis_own_sum = lane_sum(energy[...])[:1]
    picked = jnp.zeros((mine.shape[0], part_rows), f32)
    for part in range(freq_devices):
        picked = jnp.where(z == part, mine[:, part * part_rows : (part + 1) * part_rows], picked)
    for s in range(pair_dev):
        row = jnp.where(c == 0, picked[s : s + 1], picked[2 + s : 3 + s])
        row = row + mis_own_sum[:, s * part_rows : (s + 1) * part_rows]
        misfit_out[pl.ds(s, 1), :] = row * f32(1.0 / (2.0 * block * lags * freq_total))

    for t in range(stages):
        for r in (0, 1, 3, 2):
            gather_end(t, r)
            back(t, 1, lambda w: (2, r))

    lines = jnp.sum(gsum[...], axis=0, keepdims=True) * f32(1.0 / (block * math.sqrt(slot_count)))
    gsend[...] = jnp.broadcast_to(lines[:, points:], gsend.shape)
    swap_sum = remote(gsend, grecv, core_send.at[5], core_recv.at[5], other)
    swap_sum.start()
    swap_sum.wait_recv()
    row_ids = lax.broadcasted_iota(jnp.int32, (2, points), 0)
    gradient_out[...] = jnp.where(
        row_ids == c, jnp.broadcast_to(lines[:, :points], (2, points)), grecv[:2]
    )

    swap_psd.wait_send()
    for copy in swap_green:
        copy.wait_send()
    swap_ohat.wait_send()
    swap_mis.wait_send()
    swap_sum.wait_send()
    for dz in range(1, freq_devices):
        copy_z(dz).wait_send()

    def leave1(n, carry):
        copy1(n).wait_send()
        return carry

    lax.fori_loop(0, 48, leave1, 0)

    def leave2(v, carry):
        t, h, d = v // 4, (v // 2) % 2, v % 2
        copy_a(t, h, d).wait_send()
        for k in range(2):
            copy_b(t, h, d, k).wait_send()
        copy_g1(t, h, d).wait_send()
        copy_g1f(t, h, d).wait_send()
        for r in range(4):
            copy_g2(t, h, d, r).wait_send()
        for j in range(2):
            copy_g2f(t, h, d, j).wait_send()
        return carry

    lax.fori_loop(0, 8, leave2, 0)


def local(green_spectra, source_psd, pair_list, owner_map, observed):
    freq_devices = lax.axis_size("freq")
    planes, freq_dev, stations, points = green_spectra.shape
    pair_dev, block, unused_cols, lags = observed.shape
    slot_count = owner_map.shape[0]
    blocks = stations // block
    freq_total = freq_dev * freq_devices
    places = jnp.arange(slot_count, dtype=jnp.int32)
    earlier = (owner_map[None, :] < owner_map[:, None]) | (
        (owner_map[None, :] == owner_map[:, None]) & (places[None, :] < places[:, None])
    )
    slot_of_entry = jnp.sum(earlier.astype(jnp.int32), axis=1)
    hit = slot_of_entry[None, :] == places[:, None]
    ids = jnp.sum(jnp.where(hit[None], pair_list.T[:, None, :], 0), axis=2).reshape(2 * slot_count)
    table = jnp.asarray(phase_table(freq_total, lags, freq_devices))
    rows = table.shape[1]
    units = stages * 2 * 2
    dma = pltpu.SemaphoreType.DMA
    vmem = pl.BlockSpec(memory_space=pltpu.VMEM)
    anywhere = pl.BlockSpec(memory_space=pl.ANY)
    pair = (2, block, block)
    gradient, misfit = pl.pallas_call(
        functools.partial(kernel, freq_devices),
        out_shape=(
            jax.ShapeDtypeStruct((freq_dev, points), f32),
            jax.ShapeDtypeStruct((pair_dev, block // freq_devices), f32),
        ),
        in_specs=[pl.BlockSpec(memory_space=pltpu.SMEM), vmem, anywhere, anywhere, anywhere],
        out_specs=(vmem, vmem),
        scratch_shapes=[
            pltpu.VMEM((2, blocks, block, 2 * points), bf16),
            pltpu.VMEM((2, blocks, block, 2 * points), bf16),
            pltpu.VMEM((freq_dev, points), f32),
            pltpu.VMEM((pair_dev, block, block, lags), bf16),
            pltpu.VMEM((rows, lags), bf16),
            pltpu.VMEM((rows, group * lags), bf16),
            pltpu.VMEM((2 * pair_dev,) + pair, f32),
            pltpu.VMEM((pair_dev,) + pair, f32),
            pltpu.VMEM((pair_dev * (block // freq_devices), lags), f32),
            pltpu.VMEM((24 * stages,) + pair, bf16),
            pltpu.VMEM((24 * stages,) + pair, bf16),
            pltpu.VMEM((units, block, block), bf16),
            pltpu.VMEM((units, block, block), bf16),
            pltpu.VMEM((units,) + pair, bf16),
            pltpu.VMEM((units,) + pair, bf16),
            pltpu.VMEM((units, block, block), f32),
            pltpu.VMEM((slot_count,) + pair, bf16),
            pltpu.VMEM((2 * stages, block, block), f32),
            pltpu.VMEM((8, block), f32),
            pltpu.VMEM((8, block), f32),
            pltpu.VMEM((8, block), f32),
            pltpu.VMEM((freq_devices - 1, 8, block), f32),
            pltpu.VMEM((8, 2 * points), f32),
            pltpu.VMEM((8, points), f32),
            pltpu.VMEM((8, points), f32),
            dma((4,)),
            dma((6,)),
            dma((6,)),
            dma((24 * stages,)),
            dma((24 * stages,)),
            dma((units,)),
            dma((units,)),
            dma((2 * units,)),
            dma((2 * units,)),
            dma((units,)),
            dma((units,)),
            dma((units,)),
            dma((units,)),
            dma((4 * units,)),
            dma((4 * units,)),
            dma((2 * units,)),
            dma((2 * units,)),
            dma((freq_devices - 1,)),
            dma((freq_devices - 1,)),
        ],
        compiler_params=pltpu.CompilerParams(
            collective_id=0, has_side_effects=True, vmem_limit_bytes=48 * 1024 * 1024
        ),
        cost_estimate=pl.CostEstimate(
            flops=8 * slot_count * freq_dev * 2 * block * block * points,
            bytes_accessed=12 * 1024 * 1024,
            transcendentals=0,
        ),
        name="misfit_gradient",
    )(
        ids,
        source_psd,
        table,
        green_spectra.reshape(planes, freq_dev, blocks, block, points),
        observed,
    )
    return (gradient, misfit)


def solution(mesh):
    in_specs = (
        P(None, "freq", None, "grid"),
        P("freq", "grid"),
        P(),
        P(),
        P("grid", None, None, None),
    )
    out_specs = (P("freq", "grid"), P("grid", "freq"))
    return jax.shard_map(local, mesh=mesh, in_specs=in_specs, out_specs=out_specs, check_vma=False)
```

time: 478 us -> 89 us (0.19)
  waiting for transfers between devices: 186 us -> 0 us
  local copies, waits for them, and re-layouts: 128 us -> 5.03 us
  Pallas kernels: 0 us -> 81.4 us
  matrix products: 72.1 us -> 0 us
  other arithmetic: 62.1 us -> 1.71 us
  between operations: 14.1 us -> 0.66 us
  blocking collectives: 7.92 us -> 0 us
    psum x1 -> x0, waiting for transfers between devices: 124 us -> none  [local(): lax.psum(grouped.reshape(slot_count, 2, freq_dev, block_size, block_size)...]
    gather x34 -> x0, local copies, waits for them, and re-layouts: 115 us -> none  [the longest x8 33.7 us: one_group(): right_block = jnp.take(plain_blocks, block_ids[1], axis=2)]
    pallas_call x0 -> x1, Pallas kernels: none -> 81.4 us  [local(): pl.pallas_call(functools.partial(kernel, freq_devices), out_shape=(jax.Sh...]
    dot_general x34 -> x0, matrix products: 72.1 us -> none  [the longest x8 22 us: one_group(): jnp.einsum('cfsix,cfsjx->sfij', left_block, turned, preferred_element_typ...]
    all_gather x1 -> x0, waiting for transfers between devices: 54.4 us -> none  [local(): shard_piece = lax.all_gather(adjoint, 'grid', axis=0, tiled=True)]
    neg x16 -> x0, other arithmetic: 21.6 us -> none  [the longest x8 12.7 us: add_group(): -right_block[1]]
    select_n x26 -> x0, other arithmetic: 19.1 us -> none  [the longest x8 14.8 us: one_group(): right_block = jnp.take(plain_blocks, block_ids[1], axis=2)]
    dynamic_update_slice x8 -> x0, other arithmetic: 10.4 us -> none  [local(): grouped = lax.map(one_group, (left_ids, right_ids))]
  transfers between devices with their start and end apart: 3 -> 0, of which waited for: 3 -> 0; matrix products, arithmetic and copies ran while one was open for 0% -> 0% of each run, Pallas kernels for 0% -> 0%
where the time goes in v1:
time: 89 us; the launch traced here: 88.8 us
  Pallas kernels  81.4 us (91%)
  local copies, waits for them, and re-layouts  5.03 us (6%)
  other arithmetic  1.71 us (2%)
    pallas_call x1, Pallas kernels, local(): pl.pallas_call(functools.partial(kernel, freq_devices), out_shape=(jax.Sh...  81.4 us
    unnamed x8, local copies, waits for them, and re-layouts  4.95 us

profile of v1, /device:TPU:1, one launch (start us, length us, event | category | flops | bytes accessed | tf_op | source)
XLA Modules:
  0.0 88.8 jit_solution(7514316804289019991)
XLA Ops:
  0.6 0.9 %convert_reduce_fusion = s32[64]{0:T(128)S(1)} fusion(s32[64]{0:T(128)} %param.9), kind=kLoop, calls=%fused_computation.2 | loop fusion | flops 28608 | bytes 512 | tf_op jit(solution)/shard_map/reduce_sum | solution.py:568
  1.6 0.8 select_reduce_fusion
  2.4 0.1 reshape.34.ids
  2.4 0.0 copy-start
  2.4 2.2 %copy-done = bf16[2,2,2048,256]{3,2,1,0:T(8,128)(2,1)S(1)} copy-done((bf16[2,2,2048,256]{3,2,1,0:T(8,128)(2,1)S(1)}, bf16[2,2,2048,256]{3,2,1,0:T(8,128)(2,1)}, u32[]{:S(2)}) %copy-start) | copy-done | bytes 4194328
  4.6 0.0 copy-start.1
  4.6 0.7 copy-done.1
  5.3 0.0 copy-start.2
  5.3 0.9 %copy-done.2 = bf16[8,96,128]{2,1,0:T(8,128)(2,1)S(1)} copy-done((bf16[8,96,128]{2,1,0:T(8,128)(2,1)S(1)}, bf16[8,96,128]{2,1,0:T(8,128)(2,1)}, u32[]{:S(2)}) %copy-start.2) | copy-done | bytes 196632
  6.2 81.4 %misfit_gradient.1 = (f32[2,256]{1,0:T(2,128)S(1)}, f32[2,32]{1,0:T(2,128)S(1)}) custom-call(s32[128]{0:T(128)S(1)} %reshape.34.ids, f32[2,256]{1,0:T(2,128)S(1)} %copy-done.1, bf16[8,96,128]{2,1,0:T(8,128)(2,1)S(1)} %copy-done.2, bf16[2,2,16,128,256]{4,3,2,1,0:T(8,128)(2,1)S(1)} %bitcast.2, bf16[2,128,128,128]{3,2,1,0:T(8,128)(2,1)} %observed.1), custom_call_target="tpu_custom_call" | custom-call | flops 8589934592 | bytes 12582912 | tf_op jit(solution)/shard_map/misfit_gradient/pallas_call | solution.py:578
  87.7 0.6 copy.10
  88.3 0.6 copy.11
  (1 shorter events, 0.0 us)
Async XLA Ops:
  2.4 2.2 %copy-start = (bf16[2,2,2048,256]{3,2,1,0:T(8,128)(2,1)S(1)}, bf16[2,2,2048,256]{3,2,1,0:T(8,128)(2,1)}, u32[]{:S(2)}) copy-start(bf16[2,2,2048,256]{3,2,1,0:T(8,128)(2,1)} %param.6) | copy-start | bytes 12582916
  4.6 0.7 copy-start.1
  5.3 0.9 %copy-start.2 = (bf16[8,96,128]{2,1,0:T(8,128)(2,1)S(1)}, bf16[8,96,128]{2,1,0:T(8,128)(2,1)}, u32[]{:S(2)}) copy-start(bf16[8,96,128]{2,1,0:T(8,128)(2,1)} %constant.4.clone.table) | copy-start | bytes 589828

commit v2 on v1

v2 whole, which is shorter than its diff:
```python
import functools
import math

import jax
import jax.numpy as jnp
import ml_dtypes
import numpy as np
from jax import lax
from jax.experimental import pallas as pl
from jax.experimental.pallas import tpu as pltpu
from jax.sharding import PartitionSpec as P

harmonic_step = 3
side = 4
stages = 2
pieces = 3
group = 8
MESH = pl.DeviceIdType.MESH
f32 = jnp.float32
bf16 = jnp.bfloat16


def phase_table(freq_total, lag_count, freq_devices):
    freq_ids = np.arange(freq_total)[:, None]
    turns = harmonic_step * (freq_ids + 1) * np.arange(lag_count)[None, :] % lag_count
    angles = turns * (2.0 * math.pi / lag_count)
    exact = np.stack((np.cos(angles), -np.sin(angles)), axis=1)
    parts = []
    for unused in range(pieces):
        part = exact.astype(ml_dtypes.bfloat16)
        parts.append(part)
        exact = exact - part.astype(np.float64)
    table = np.stack(parts).reshape(pieces, freq_devices, 2, 2, lag_count)
    both = np.stack((table, table[:, :, ::-1]), axis=2)
    both = both.transpose(1, 2, 0, 3, 4, 5).reshape(freq_devices * 2, pieces * 4, lag_count)
    return np.repeat(both, group, axis=1)


def kernel(
    freq_devices,
    owner,
    pairs,
    psd_hbm,
    table,
    green,
    observed,
    gradient_out,
    misfit_out,
    gbuf,
    wbuf,
    psd,
    psd_other,
    owner_row,
    pair_rows,
    ids_row,
    ids,
    obs,
    phi,
    spread,
    ohat,
    ohat_send,
    energy,
    send1,
    recv1,
    send_a,
    recv_a,
    send_b,
    recv_b,
    keep,
    own_sum,
    abuf,
    total,
    mis_own,
    mis_other,
    mis_pair,
    mis_freq,
    gsum,
    gsend,
    grecv,
    local_sem,
    core_send,
    core_recv,
    green_send,
    green_recv,
    one_send,
    one_recv,
    a_send,
    a_recv,
    b_send,
    b_recv,
    g1_send,
    g1_recv,
    g1f_send,
    g1f_recv,
    g2_send,
    g2_recv,
    g2f_send,
    g2f_recv,
    z_send,
    z_recv,
):
    z = lax.axis_index("freq")
    g = lax.axis_index("grid")
    c = g % 2
    x = (g // 2) % side
    y = g // (2 * side)
    other = g + 1 - 2 * c
    points = psd_hbm.shape[1]
    pair_dev, block, unused_cols, lags = observed.shape
    freq_total = 2 * freq_devices
    slot_count = 2 * side * side * pair_dev
    root_scale = 1.0 / math.sqrt(points * 2 * side * side)

    def neighbour(axis, d):
        step = 1 + 2 * d
        nx = (x + (1 - axis) * step) % side
        ny = (y + axis * step) % side
        return (ny * side + nx) * 2 + c

    def slot_of(t, h, o, r):
        sx = (x + (1 - h) * o + h * r) % side
        sy = (y + h * o + (1 - h) * r) % side
        return (sy * side + sx) * 4 + h * 2 + t

    def lane(d, j):
        return (1 - d) * (2 - 2 * j) + d * (1 + 2 * j)

    def lane_place(r):
        return ((r + 1) // 2 + 1) % 2

    def remote(src, dst, send, recv, device):
        return pltpu.make_async_remote_copy(
            src_ref=src, dst_ref=dst, send_sem=send, recv_sem=recv,
            device_id={"grid": device}, device_id_type=MESH,
        )

    barrier = pltpu.get_barrier_semaphore()
    friends = [{"grid": other}]
    for axis in range(2):
        for d in range(2):
            friends.append({"grid": neighbour(axis, d)})
    for dz in range(1, freq_devices):
        friends.append({"freq": (z + dz) % freq_devices})
    for friend in friends:
        pl.semaphore_signal(barrier, inc=1, device_id=friend, device_id_type=MESH)

    own_points = pl.ds(0, points)
    other_points = pl.ds(points, points)
    load_owner = pltpu.make_async_copy(owner, owner_row, local_sem.at[4])
    load_pairs = pltpu.make_async_copy(pairs, pair_rows, local_sem.at[5])
    load_psd = pltpu.make_async_copy(psd_hbm, psd, local_sem.at[6])
    load_green = [
        pltpu.make_async_copy(green.at[k, c], gbuf.at[k, :, :, own_points], local_sem.at[k])
        for k in range(2)
    ]
    load_table = pltpu.make_async_copy(table.at[z * 2 + c], phi, local_sem.at[2])
    load_obs = pltpu.make_async_copy(observed, obs, local_sem.at[3])
    load_owner.start()
    load_pairs.start()
    load_psd.start()
    for copy in load_green:
        copy.start()
    load_table.start()
    pl.semaphore_wait(barrier, len(friends))

    swap_psd = remote(psd_hbm, psd_other, core_send.at[2], core_recv.at[2], other)
    half = gbuf.shape[1] // 2

    def swap_green(n):
        k, some = n // 2, pl.ds(n % 2 * half, half)
        return remote(
            green.at[k, 1 - c, some], gbuf.at[k, some, :, other_points],
            green_send.at[n], green_recv.at[n], other,
        )

    swap_psd.start()
    for n in range(4):
        swap_green(n).start()
    load_obs.start()

    def weigh(k, first, count, where, row):
        def body(b, carry):
            for i in range(4):
                place = first + 4 * b + i
                wbuf[k, place, :, where] = (gbuf[k, place, :, where].astype(f32) * row).astype(bf16)
            return carry

        lax.fori_loop(0, count // 4, body, 0)

    load_owner.wait()
    load_pairs.wait()
    square = (slot_count, slot_count)
    across = lax.broadcasted_iota(jnp.int32, square, 1)
    along = lax.broadcasted_iota(jnp.int32, square, 0)

    def down(row):
        return jnp.sum(jnp.where(across == along, jnp.broadcast_to(row, square), 0), axis=1, keepdims=True)

    their_owner = jnp.broadcast_to(owner_row[...], square)
    my_owner = down(owner_row[...])
    earlier = (their_owner < my_owner) | ((their_owner == my_owner) & (across < along))
    ids_row[...] = jnp.zeros_like(ids_row)
    entry_slot = jnp.sum(jnp.where(earlier, 1, 0), axis=1, keepdims=True)
    hit = entry_slot == across
    for k in range(2):
        chosen = jnp.where(hit, down(pair_rows[pl.ds(k, 1), :]), 0)
        ids_row[pl.ds(k, 1), pl.ds(0, slot_count)] = jnp.sum(chosen, axis=0, keepdims=True)
    move_ids = pltpu.make_async_copy(ids_row, ids, local_sem.at[7])
    move_ids.start()

    load_psd.wait()
    own_row = psd[pl.ds(c, 1), :]
    for k in range(2):
        load_green[k].wait()
        weigh(k, 0, 2 * half, own_points, own_row)

    load_table.wait()
    rows = phi.shape[0]
    row_in_group = lax.broadcasted_iota(jnp.int32, (rows, lags), 0) % group
    phi_values = phi[...].astype(f32)
    for i in range(group):
        spread[:, pl.ds(i * lags, lags)] = jnp.where(row_in_group == i, phi_values, 0.0).astype(bf16)

    recv1[48] = jnp.zeros_like(recv1[48])
    gsum[...] = jnp.zeros_like(gsum)
    mis_own[...] = jnp.zeros_like(mis_own)
    move_ids.wait()
    swap_psd.wait_recv()
    other_row = psd_other[pl.ds(c, 1), :]
    for n in range(4):
        swap_green(n).wait_recv()
        weigh(n // 2, n % 2 * half, half, other_points, other_row)

    def units(slots):
        pairs_of = []
        for slot in slots:
            left = wbuf[:, ids[0, slot]].reshape(2 * block, 2 * points)
            right = gbuf[:, ids[1, slot]].reshape(2 * block, 2 * points)
            acc = lax.dot_general(left, right, (((1,), (1,)), ((), ())), preferred_element_type=f32)
            real = acc[:block, :block] + acc[block:, block:]
            imag = acc[block:, :block] - acc[:block, block:]
            pairs_of.append((real, imag))
        return pairs_of

    def copy1(n):
        u = n % 8
        return remote(
            send1.at[n], recv1.at[n], one_send.at[n], one_recv.at[n], neighbour(u % 2, (u // 2) % 2)
        )

    def first_ring(i, carry):
        part, t, j = i // 4, (i % 4) // 2, i % 2
        through = part == 1
        role = jnp.where(through, 2, part // 2)
        first = t * 24 + role * 8 + j * 4

        @pl.when(through)
        def _():
            project(i - 4)
            for u in range(4):
                copy1(first - 16 + u).wait_recv()

        slots = []
        for u in range(4):
            h, d = u % 2, u // 2
            o = jnp.where(part == 0, 2, 1 + 2 * d)
            r = jnp.where(part == 2, lane(1 - d, j), lane(d, j))
            slots.append(slot_of(t, h, o, r))
        for u, values in enumerate(units(slots)):
            n = first + u
            with_n = jnp.where(through, n - 16, 48)
            for k in range(2):
                send1[n, k] = (values[k] + recv1[with_n, k].astype(f32)).astype(bf16)
        for u in range(4):
            copy1(first + u).start()
        return carry

    def arrival1(t, h, d, r):
        role = 2 - (r + d) % 2
        return t * 24 + role * 8 + lane_place(r) * 4 + d * 2 + h

    def line_sums(t, wanted):
        for h, r in wanted:
            for d in range(2):
                copy1(arrival1(t, h, d, r)).wait_recv()
        sums = []
        for (h, r), values in zip(wanted, units([slot_of(t, h, 0, r) for h, r in wanted])):
            arrived = [recv1[arrival1(t, h, d, r)].astype(f32) for d in range(2)]
            sums.append([values[k] + (arrived[0][k] + arrived[1][k]) for k in range(2)])
        return sums

    def place(t, h, d):
        return (t * 2 + h) * 2 + d

    def copy_a(t, h, d):
        i = place(t, h, d)
        return remote(send_a.at[i], recv_a.at[i], a_send.at[i], a_recv.at[i], neighbour(1 - h, d))

    def copy_b(t, h, d, k):
        i = place(t, h, d)
        return remote(
            send_b.at[i, k], recv_b.at[i, k], b_send.at[i * 2 + k], b_recv.at[i * 2 + k],
            neighbour(1 - h, d),
        )

    def second_ring_open(t, carry):
        for h, values in enumerate(line_sums(t, [(0, 2), (1, 2)])):
            for d in range(2):
                send_a[place(t, h, d)] = values[d].astype(bf16)
                copy_a(t, h, d).start()
        wanted = [(h, 1 + 2 * d) for d in range(2) for h in range(2)]
        for (h, r), values in zip(wanted, line_sums(t, wanted)):
            d = r // 2
            i = place(t, h, d)
            send_b[i, 1 - d] = values[1 - d].astype(bf16)
            copy_b(t, h, d, 1 - d).start()
            keep[i] = values[d]
        return carry

    def own_part(t, carry):
        for h, values in enumerate(line_sums(t, [(0, 0), (1, 0)])):
            for k in range(2):
                own_sum[t * 2 + h, k] = values[k]
        return carry

    def second_ring_close(t, carry):
        for d in range(2):
            for h in range(2):
                i = place(t, h, d)
                copy_a(t, h, d).wait_recv()
                send_b[i, d] = (keep[i] + recv_a[i].astype(f32)).astype(bf16)
                copy_b(t, h, d, d).start()
        return carry

    def copy_g1(t, h, d):
        s, i = slot_of(t, h, 0, 0), place(t, h, d)
        return remote(abuf.at[s], abuf.at[s], g1_send.at[i], g1_recv.at[i], neighbour(1 - h, d))

    def copy_g1f(t, h, d):
        s, i = slot_of(t, h, 0, 3 - 2 * d), place(t, h, d)
        return remote(abuf.at[s, d], abuf.at[s, d], g1f_send.at[i], g1f_recv.at[i], neighbour(1 - h, d))

    def copy_g2(t, h, d, r):
        s, i = slot_of(t, h, 0, r), place(t, h, d) * 4 + r
        return remote(abuf.at[s], abuf.at[s], g2_send.at[i], g2_recv.at[i], neighbour(h, d))

    def copy_g2f(t, h, d, j):
        s, i = slot_of(t, h, 3 - 2 * d, lane(d, j)), place(t, h, d) * 2 + j
        return remote(abuf.at[s], abuf.at[s], g2f_send.at[i], g2f_recv.at[i], neighbour(h, d))

    ones = jnp.ones((8, block), f32)

    def lane_sum(values):
        return lax.dot_general(
            ones[:, : values.shape[1]], values, (((1,), (1,)), ((), ())),
            precision=lax.Precision.HIGHEST, preferred_element_type=f32,
        )

    def own_adjoint(t, carry):
        for h in range(2):
            for d in range(2):
                for k in range(2):
                    copy_b(t, h, d, k).wait_recv()
            s, q = slot_of(t, h, 0, 0), h * 2 + t
            kept = jnp.zeros((block, block), f32)
            for k in range(2):
                value = own_sum[t * 2 + h, k]
                for d in range(2):
                    value = value + recv_b[place(t, h, d), k].astype(f32)
                cross = value * f32(root_scale)
                seen = ohat[q, k]
                abuf[s, k] = (0.5 * cross - seen * f32(1.0 / lags)).astype(bf16)
                kept = kept + cross * (f32(lags / 2) * cross - 2.0 * seen)
            for d in range(2):
                copy_g1(t, h, d).start()
            for d in range(2):
                copy_g2(t, h, d, 0).start()
            total[q] = kept
        return carry

    def gather_1(t):
        def body(v, carry):
            h, d = v % 2, v // 2
            copy_g1(t, h, d).wait_recv()
            copy_g1f(t, h, d).start()
            for side_d in range(2):
                copy_g2(t, h, side_d, 3 - 2 * d).start()
            return carry

        lax.fori_loop(0, 4, body, 0)

    def gather_2(t):
        def body(h, carry):
            for d in range(2):
                copy_g1f(t, h, d).wait_recv()
            for d in range(2):
                copy_g2(t, h, d, 2).start()
            return carry

        lax.fori_loop(0, 2, body, 0)

    def gather_lane(t, r):
        e = r % 2
        j = lane_place(r)

        def body(h, carry):
            copy_g2(t, h, e, r).wait_recv()
            copy_g2f(t, h, e, j).start()
            copy_g2(t, h, 1 - e, r).wait_recv()
            return carry

        lax.fori_loop(0, 2, body, 0)

    def gather_end(t, r):
        def body(h, carry):
            copy_g2f(t, h, r % 2, lane_place(r)).wait_recv()
            return carry

        lax.fori_loop(0, 2, body, 0)

    def back(slots, carry):
        for s in slots:
            weights = abuf[s]
            top = jnp.concatenate((weights[0], -weights[1]), axis=1)
            low = jnp.concatenate((weights[1], weights[0]), axis=1)
            right = gbuf[:, ids[1, s]].reshape(2 * block, 2 * points)
            moved = jnp.dot(
                jnp.concatenate((top, low), axis=0), right, preferred_element_type=f32
            )
            left = gbuf[:, ids[0, s]].reshape(2 * block, 2 * points).astype(f32)
            carry = carry + jnp.sum((moved * left).reshape(2 * block // 8, 8, 2 * points), axis=0)
        return carry

    def project(quarter):
        @pl.when(quarter == 0)
        def _():
            load_obs.wait()

        chunks = block // group // 4

        def body(i, carry):
            first = pl.multiple_of((quarter * chunks + i) * group, group)
            seen = jnp.concatenate(
                [
                    jnp.concatenate([obs[s, first + k] for k in range(group)], axis=1)
                    for s in range(pair_dev)
                ],
                axis=0,
            )
            out = lax.dot_general(
                spread[...], seen, (((1,), (1,)), ((), ())), preferred_element_type=f32
            )
            out = jnp.sum(out.reshape(pieces, 4 * group, pair_dev * block), axis=0)
            for s in range(pair_dev):
                for k in range(2):
                    cols = slice(s * block, (s + 1) * block)
                    ohat[2 * c + s, k, pl.ds(first, group), :] = out[k * group : (k + 1) * group, cols]
                    ohat_send[s, k, pl.ds(first, group), :] = out[(2 + k) * group : (3 + k) * group, cols]
            return carry

        lax.fori_loop(0, chunks, body, 0, unroll=2)

    swap_ohat = remote(
        ohat_send, ohat.at[pl.ds(2 * c, 2)], core_send.at[3], core_recv.at[3], other
    )
    part_rows = block // freq_devices

    def energies():
        def body(i, carry):
            for s in range(pair_dev):
                seen = obs[s, z * part_rows + i].astype(f32)
                energy[pl.ds(s * part_rows + i, 1), :] = jnp.sum(seen * seen, axis=0, keepdims=True)
            return carry

        lax.fori_loop(0, part_rows, body, 0)

    swap_mis = remote(mis_own, mis_other, core_send.at[4], core_recv.at[4], other)

    def copy_z(dz):
        return pltpu.make_async_remote_copy(
            src_ref=mis_pair, dst_ref=mis_freq.at[dz - 1],
            send_sem=z_send.at[dz - 1], recv_sem=z_recv.at[dz - 1],
            device_id={"freq": (z + dz) % freq_devices}, device_id_type=MESH,
        )

    def misfit_parts():
        for q in range(2 * stages):
            mis_own[pl.ds(q, 1), :] = lane_sum(total[q])[:1]
        swap_mis.start()

    def misfit_sums():
        swap_mis.wait_recv()
        mis_pair[...] = mis_own[...] + mis_other[...]
        for dz in range(1, freq_devices):
            copy_z(dz).start()

    def misfit_end():
        mine = mis_pair[...]
        for dz in range(1, freq_devices):
            copy_z(dz).wait_recv()
            mine = mine + mis_freq[dz - 1]
        from_observed = lane_sum(energy[...])[:1]
        picked = jnp.zeros((mine.shape[0], part_rows), f32)
        for part in range(freq_devices):
            picked = jnp.where(z == part, mine[:, part * part_rows : (part + 1) * part_rows], picked)
        for s in range(pair_dev):
            row = jnp.where(c == 0, picked[s : s + 1], picked[2 + s : 3 + s])
            row = row + from_observed[:, s * part_rows : (s + 1) * part_rows]
            misfit_out[pl.ds(s, 1), :] = row * f32(1.0 / (2.0 * block * lags * freq_total))

    def leave1(n, carry):
        copy1(n).wait_send()
        return carry

    def leave2(v, carry):
        t, h, d = v // 4, (v // 2) % 2, v % 2
        copy_a(t, h, d).wait_send()
        for k in range(2):
            copy_b(t, h, d, k).wait_send()
        copy_g1(t, h, d).wait_send()
        return carry

    def leave3(v, carry):
        t, h, d = v // 4, (v // 2) % 2, v % 2
        copy_g1f(t, h, d).wait_send()
        for r in range(4):
            copy_g2(t, h, d, r).wait_send()
        for j in range(2):
            copy_g2f(t, h, d, j).wait_send()
        return carry

    lax.fori_loop(0, 12, first_ring, 0)
    swap_ohat.start()
    energies()
    lax.fori_loop(0, 2, second_ring_open, 0)
    lax.fori_loop(0, 2, own_part, 0)
    lax.fori_loop(0, 2, second_ring_close, 0)
    swap_ohat.wait_recv()
    lax.fori_loop(0, 2, own_adjoint, 0)

    steps = [
        ([], (0, 1), (0, 0), (0, 0)),
        ([(gather_1, 0)], (0, 0), (0, 0), (1, 2)),
        ([(gather_lane, 0, 0)], (0, 0), (1, 2), (0, 0)),
        ([(gather_1, 1)], (1, 0), (0, 0), (1, 2)),
        ([(gather_lane, 1, 0)], (1, 0), (1, 2), (0, 0)),
        ([(gather_2, 0), (gather_lane, 0, 1)], (0, 0), (1, 2), (1, 0)),
        ([(gather_lane, 0, 3)], (0, 0), (1, 2), (3, 0)),
        ([(gather_2, 1), (misfit_parts,)], (0, 1), (0, 0), (2, 0)),
        ([(gather_end, 0, 0), (gather_end, 1, 0)], (0, 1), (2, 0), (0, 0)),
        ([(gather_lane, 1, 1), (misfit_sums,)], (1, 0), (1, 2), (1, 0)),
        ([(gather_lane, 1, 3)], (1, 0), (1, 2), (3, 0)),
        ([(gather_lane, 0, 2)], (0, 0), (1, 2), (2, 0)),
        ([(gather_lane, 1, 2), (misfit_end,)], (1, 0), (1, 2), (2, 0)),
        ([(gather_end, 0, 1), (gather_end, 1, 1)], (0, 1), (2, 0), (1, 0)),
        ([(gather_end, 0, 3), (gather_end, 1, 3)], (0, 1), (2, 0), (3, 0)),
        ([(gather_end, 0, 2), (gather_end, 1, 2)], (0, 1), (2, 0), (2, 0)),
    ]

    def choose(i, values):
        chosen = values[0]
        for n in range(1, len(values)):
            chosen = jnp.where(i >= n, values[n], chosen) if values[n] != values[n - 1] else chosen
        return chosen

    def gather_step(i, carry):
        for n, step in enumerate(steps):
            if step[0]:
                @pl.when(i == n)
                def _(actions=tuple(step[0])):
                    for action in actions:
                        action[0](*action[1:])

        slots = []
        for u in range(4):
            t, o, r = (
                choose(i, [step[part][0] + u // 2 * step[part][1] for step in steps]) for part in (1, 2, 3)
            )
            slots.append(slot_of(t, u % 2, o, r))
        return back(slots, carry)

    gsum[...] = lax.fori_loop(0, len(steps), gather_step, gsum[...])

    lines = jnp.sum(gsum[...], axis=0, keepdims=True) * f32(1.0 / (block * math.sqrt(slot_count)))
    gsend[...] = jnp.broadcast_to(lines[:, points:], gsend.shape)
    swap_sum = remote(gsend, grecv, core_send.at[5], core_recv.at[5], other)
    swap_sum.start()
    swap_sum.wait_recv()
    row_ids = lax.broadcasted_iota(jnp.int32, (2, points), 0)
    gradient_out[...] = jnp.where(
        row_ids == c, jnp.broadcast_to(lines[:, :points], (2, points)), grecv[:2]
    )

    swap_psd.wait_send()
    for n in range(4):
        swap_green(n).wait_send()
    swap_ohat.wait_send()
    swap_mis.wait_send()
    swap_sum.wait_send()
    for dz in range(1, freq_devices):
        copy_z(dz).wait_send()
    lax.fori_loop(0, 48, leave1, 0)
    lax.fori_loop(0, 8, leave2, 0)
    lax.fori_loop(0, 8, leave3, 0)


def local(green_spectra, source_psd, pair_list, owner_map, observed):
    freq_devices = lax.axis_size("freq")
    planes, freq_dev, stations, points = green_spectra.shape
    pair_dev, block, unused_cols, lags = observed.shape
    slot_count = owner_map.shape[0]
    blocks = stations // block
    freq_total = freq_dev * freq_devices
    table = jnp.asarray(phase_table(freq_total, lags, freq_devices))
    rows = table.shape[1]
    units = stages * 2 * 2
    dma = pltpu.SemaphoreType.DMA
    vmem = pl.BlockSpec(memory_space=pltpu.VMEM)
    hbm = pl.BlockSpec(memory_space=pltpu.HBM)
    pair = (2, block, block)
    gradient, misfit = pl.pallas_call(
        functools.partial(kernel, freq_devices),
        out_shape=(
            jax.ShapeDtypeStruct((freq_dev, points), f32),
            jax.ShapeDtypeStruct((pair_dev, block // freq_devices), f32),
        ),
        in_specs=[hbm] * 6,
        out_specs=(vmem, vmem),
        scratch_shapes=[
            pltpu.VMEM((2, blocks, block, 2 * points), bf16),
            pltpu.VMEM((2, blocks, block, 2 * points), bf16),
            pltpu.VMEM((freq_dev, points), f32),
            pltpu.VMEM((freq_dev, points), f32),
            pltpu.VMEM((1, slot_count), jnp.int32),
            pltpu.VMEM((2, slot_count), jnp.int32),
            pltpu.VMEM((8, 128), jnp.int32),
            pltpu.SMEM((8, 128), jnp.int32),
            pltpu.VMEM((pair_dev, block, block, lags), bf16),
            pltpu.VMEM((rows, lags), bf16),
            pltpu.VMEM((rows, group * lags), bf16),
            pltpu.VMEM((2 * pair_dev,) + pair, f32),
            pltpu.VMEM((pair_dev,) + pair, f32),
            pltpu.VMEM((pair_dev * (block // freq_devices), lags), f32),
            pltpu.VMEM((24 * stages,) + pair, bf16),
            pltpu.VMEM((24 * stages + 1,) + pair, bf16),
            pltpu.VMEM((units, block, block), bf16),
            pltpu.VMEM((units, block, block), bf16),
            pltpu.VMEM((units,) + pair, bf16),
            pltpu.VMEM((units,) + pair, bf16),
            pltpu.VMEM((units, block, block), f32),
            pltpu.VMEM((2 * stages,) + pair, f32),
            pltpu.VMEM((slot_count,) + pair, bf16),
            pltpu.VMEM((2 * stages, block, block), f32),
            pltpu.VMEM((8, block), f32),
            pltpu.VMEM((8, block), f32),
            pltpu.VMEM((8, block), f32),
            pltpu.VMEM((freq_devices - 1, 8, block), f32),
            pltpu.VMEM((8, 2 * points), f32),
            pltpu.VMEM((8, points), f32),
            pltpu.VMEM((8, points), f32),
            dma((8,)),
            dma((6,)),
            dma((6,)),
            dma((4,)),
            dma((4,)),
            dma((24 * stages,)),
            dma((24 * stages,)),
            dma((units,)),
            dma((units,)),
            dma((2 * units,)),
            dma((2 * units,)),
            dma((units,)),
            dma((units,)),
            dma((units,)),
            dma((units,)),
            dma((4 * units,)),
            dma((4 * units,)),
            dma((2 * units,)),
            dma((2 * units,)),
            dma((freq_devices - 1,)),
            dma((freq_devices - 1,)),
        ],
        compiler_params=pltpu.CompilerParams(
            collective_id=0, has_side_effects=True, vmem_limit_bytes=60 * 1024 * 1024
        ),
        cost_estimate=pl.CostEstimate(
            flops=8 * slot_count * freq_dev * 2 * block * block * points,
            bytes_accessed=12 * 1024 * 1024,
            transcendentals=0,
        ),
        name="misfit_gradient",
    )(
        owner_map.reshape(1, slot_count),
        pair_list.T,
        source_psd,
        table,
        green_spectra.reshape(planes, freq_dev, blocks, block, points),
        observed,
    )
    return (gradient, misfit)


def solution(mesh):
    in_specs = (
        P(None, "freq", None, "grid"),
        P("freq", "grid"),
        P(),
        P(),
        P("grid", None, None, None),
    )
    out_specs = (P("freq", "grid"), P("grid", "freq"))
    return jax.shard_map(local, mesh=mesh, in_specs=in_specs, out_specs=out_specs, check_vma=False)
```

time: 89 us -> 70.4 us (0.79)
  Pallas kernels: 81.4 us -> 67.2 us
  local copies, waits for them, and re-layouts: 5.03 us -> 2.46 us
  other arithmetic: 1.71 us -> 0 us
    pallas_call x1, Pallas kernels: 81.4 us -> 67.2 us  [local(): pl.pallas_call(functools.partial(kernel, freq_devices), out_shape=(jax.Sh...]
    unnamed x8 -> x2, local copies, waits for them, and re-layouts: 4.95 us -> 2.46 us
    reduce_sum x2 -> x0, other arithmetic: 1.7 us -> none  [the longest x1 0.91 us: local(): slot_of_entry = jnp.sum(earlier.astype(jnp.int32), axis=1)]
where the time goes in v2:
time: 70.4 us; the launch traced here: 70.3 us
  Pallas kernels  67.2 us (95%)
  local copies, waits for them, and re-layouts  2.46 us (3%)
    pallas_call x1, Pallas kernels, local(): pl.pallas_call(functools.partial(kernel, freq_devices), out_shape=(jax.Sh...  67.2 us
    unnamed x2, local copies, waits for them, and re-layouts  2.46 us

profile of v2, /device:TPU:1, one launch (start us, length us, event | category | flops | bytes accessed | tf_op | source)
XLA Modules:
  0.0 70.3 jit_solution(8836282888509070344)
XLA Ops:
  0.6 67.2 %misfit_gradient.1 = (f32[2,256]{1,0:T(2,128)}, f32[2,32]{1,0:T(2,128)}) custom-call(s32[1,64]{1,0:T(1,128)} %bitcast.5, s32[2,64]{1,0:T(2,128)} %bitcast.4, f32[2,256]{1,0:T(2,128)} %psd_hbm.1, bf16[8,96,128]{2,1,0:T(8,128)(2,1)} %constant.2.clone.table, bf16[2,2,16,128,256]{4,3,2,1,0:T(8,128)(2,1)} %bitcast.3, bf16[2,128,128,128]{3,2,1,0:T(8,128)(2,1)} %observed.1), custom_call_target="tpu_custom_call" | custom-call | flops 8589934592 | bytes 12582912 | tf_op jit(solution)/shard_map/misfit_gradient/pallas_call | solution.py:621
  67.8 1.2 %copy.10 = f32[2,256]{1,0:T(2,128)} copy(f32[2,256]{1,0:T(2,128)} %get-tuple-element.4) | data formatting | bytes 4096
  69.1 1.2 %copy.11 = f32[2,32]{1,0:T(2,128)} copy(f32[2,32]{1,0:T(2,128)} %get-tuple-element.5) | data formatting | bytes 512

commit v3 on v2

--- a/solution.py
+++ b/solution.py
@@ -88,16 +88,14 @@
     a_recv,
     b_send,
     b_recv,
-    g1_send,
+    g_send,
     g1_recv,
-    g1f_send,
     g1f_recv,
-    g2_send,
     g2_recv,
-    g2f_send,
     g2f_recv,
     z_send,
     z_recv,
+    z_here,
 ):
     z = lax.axis_index("freq")
     g = lax.axis_index("grid")
@@ -139,10 +137,14 @@
     for axis in range(2):
         for d in range(2):
             friends.append({"grid": neighbour(axis, d)})
-    for dz in range(1, freq_devices):
-        friends.append({"freq": (z + dz) % freq_devices})
     for friend in friends:
         pl.semaphore_signal(barrier, inc=1, device_id=friend, device_id_type=MESH)
+    for dz in range(1, freq_devices):
+
+        @pl.when(z + dz < freq_devices)
+        def _():
+            pl.semaphore_signal(barrier, inc=1, device_id={"freq": z + dz}, device_id_type=MESH)
+
 
     own_points = pl.ds(0, points)
     other_points = pl.ds(points, points)
@@ -161,7 +163,13 @@
     for copy in load_green:
         copy.start()
     load_table.start()
-    pl.semaphore_wait(barrier, len(friends))
+    pl.semaphore_wait(barrier, len(friends) + z)
+    for dz in range(1, freq_devices):
+
+        @pl.when(z >= dz)
+        def _():
+            pl.semaphore_signal(z_here, inc=1, device_id={"freq": z - dz}, device_id_type=MESH)
+
 
     swap_psd = remote(psd_hbm, psd_other, core_send.at[2], core_recv.at[2], other)
     half = gbuf.shape[1] // 2
@@ -170,7 +178,7 @@
         k, some = n // 2, pl.ds(n % 2 * half, half)
         return remote(
             green.at[k, 1 - c, some], gbuf.at[k, some, :, other_points],
-            green_send.at[n], green_recv.at[n], other,
+            green_send.at[0], green_recv.at[n], other,
         )
 
     swap_psd.start()
@@ -243,10 +251,18 @@
         return pairs_of
 
     def copy1(n):
-        u = n % 8
-        return remote(
-            send1.at[n], recv1.at[n], one_send.at[n], one_recv.at[n], neighbour(u % 2, (u // 2) % 2)
-        )
+        t, role, u = n // 24, (n % 24) // 8, n % 8
+        h, d, j = u % 2, (u // 2) % 2, u // 4
+        r = jnp.where(role == 1, lane(1 - d, j), lane(d, j))
+        i = jnp.where(role == 0, t * 2 + j, 4 + t * 4 + r)
+        return remote(send1.at[n], recv1.at[n], one_send.at[0], one_recv.at[i], neighbour(h, d))
+
+    def wait_all(buffer, count, semaphore):
+        some = buffer.at[pl.ds(0, count)]
+        pltpu.make_async_copy(some, some, semaphore).wait()
+
+    def wait1(i):
+        wait_all(recv1, 4, one_recv.at[i])
 
     def first_ring(i, carry):
         part, t, j = i // 4, (i % 4) // 2, i % 2
@@ -257,8 +273,7 @@
         @pl.when(through)
         def _():
             project(i - 4)
-            for u in range(4):
-                copy1(first - 16 + u).wait_recv()
+            wait1(t * 2 + j)
 
         slots = []
         for u in range(4):
@@ -280,9 +295,8 @@
         return t * 24 + role * 8 + lane_place(r) * 4 + d * 2 + h
 
     def line_sums(t, wanted):
-        for h, r in wanted:
-            for d in range(2):
-                copy1(arrival1(t, h, d, r)).wait_recv()
+        for r in sorted({r for h, r in wanted}):
+            wait1(4 + t * 4 + r)
         sums = []
         for (h, r), values in zip(wanted, units([slot_of(t, h, 0, r) for h, r in wanted])):
             arrived = [recv1[arrival1(t, h, d, r)].astype(f32) for d in range(2)]
@@ -294,13 +308,12 @@
 
     def copy_a(t, h, d):
         i = place(t, h, d)
-        return remote(send_a.at[i], recv_a.at[i], a_send.at[i], a_recv.at[i], neighbour(1 - h, d))
+        return remote(send_a.at[i], recv_a.at[i], a_send.at[0], a_recv.at[t], neighbour(1 - h, d))
 
     def copy_b(t, h, d, k):
         i = place(t, h, d)
         return remote(
-            send_b.at[i, k], recv_b.at[i, k], b_send.at[i * 2 + k], b_recv.at[i * 2 + k],
-            neighbour(1 - h, d),
+            send_b.at[i, k], recv_b.at[i, k], b_send.at[0], b_recv.at[t], neighbour(1 - h, d)
         )
 
     def second_ring_open(t, carry):
@@ -324,29 +337,30 @@
         return carry
 
     def second_ring_close(t, carry):
+        wait_all(recv_a, 4, a_recv.at[t])
         for d in range(2):
             for h in range(2):
                 i = place(t, h, d)
-                copy_a(t, h, d).wait_recv()
                 send_b[i, d] = (keep[i] + recv_a[i].astype(f32)).astype(bf16)
                 copy_b(t, h, d, d).start()
         return carry
 
     def copy_g1(t, h, d):
-        s, i = slot_of(t, h, 0, 0), place(t, h, d)
-        return remote(abuf.at[s], abuf.at[s], g1_send.at[i], g1_recv.at[i], neighbour(1 - h, d))
+        s = slot_of(t, h, 0, 0)
+        return remote(abuf.at[s], abuf.at[s], g_send.at[0], g1_recv.at[t], neighbour(1 - h, d))
 
     def copy_g1f(t, h, d):
-        s, i = slot_of(t, h, 0, 3 - 2 * d), place(t, h, d)
-        return remote(abuf.at[s, d], abuf.at[s, d], g1f_send.at[i], g1f_recv.at[i], neighbour(1 - h, d))
+        s = slot_of(t, h, 0, 3 - 2 * d)
+        return remote(abuf.at[s, d], abuf.at[s, d], g_send.at[0], g1f_recv.at[t], neighbour(1 - h, d))
 
     def copy_g2(t, h, d, r):
-        s, i = slot_of(t, h, 0, r), place(t, h, d) * 4 + r
-        return remote(abuf.at[s], abuf.at[s], g2_send.at[i], g2_recv.at[i], neighbour(h, d))
+        s = slot_of(t, h, 0, r)
+        return remote(abuf.at[s], abuf.at[s], g_send.at[0], g2_recv.at[t * 4 + r], neighbour(h, d))
 
     def copy_g2f(t, h, d, j):
-        s, i = slot_of(t, h, 3 - 2 * d, lane(d, j)), place(t, h, d) * 2 + j
-        return remote(abuf.at[s], abuf.at[s], g2f_send.at[i], g2f_recv.at[i], neighbour(h, d))
+        r = lane(d, j)
+        s = slot_of(t, h, 3 - 2 * d, r)
+        return remote(abuf.at[s], abuf.at[s], g_send.at[0], g2f_recv.at[r], neighbour(h, d))
 
     ones = jnp.ones((8, block), f32)
 
@@ -357,10 +371,8 @@
         )
 
     def own_adjoint(t, carry):
+        wait_all(recv_b, 4, b_recv.at[t])
         for h in range(2):
-            for d in range(2):
-                for k in range(2):
-                    copy_b(t, h, d, k).wait_recv()
             s, q = slot_of(t, h, 0, 0), h * 2 + t
             kept = jnp.zeros((block, block), f32)
             for k in range(2):
@@ -379,9 +391,10 @@
         return carry
 
     def gather_1(t):
+        wait_all(abuf, 4, g1_recv.at[t])
+
         def body(v, carry):
             h, d = v % 2, v // 2
-            copy_g1(t, h, d).wait_recv()
             copy_g1f(t, h, d).start()
             for side_d in range(2):
                 copy_g2(t, h, side_d, 3 - 2 * d).start()
@@ -390,33 +403,18 @@
         lax.fori_loop(0, 4, body, 0)
 
     def gather_2(t):
-        def body(h, carry):
-            for d in range(2):
-                copy_g1f(t, h, d).wait_recv()
+        wait_all(abuf, 2, g1f_recv.at[t])
+        for h in range(2):
             for d in range(2):
                 copy_g2(t, h, d, 2).start()
-            return carry
-
-        lax.fori_loop(0, 2, body, 0)
 
     def gather_lane(t, r):
-        e = r % 2
-        j = lane_place(r)
-
-        def body(h, carry):
-            copy_g2(t, h, e, r).wait_recv()
-            copy_g2f(t, h, e, j).start()
-            copy_g2(t, h, 1 - e, r).wait_recv()
-            return carry
-
-        lax.fori_loop(0, 2, body, 0)
-
-    def gather_end(t, r):
-        def body(h, carry):
-            copy_g2f(t, h, r % 2, lane_place(r)).wait_recv()
-            return carry
-
-        lax.fori_loop(0, 2, body, 0)
+        wait_all(abuf, 4, g2_recv.at[t * 4 + r])
+        for h in range(2):
+            copy_g2f(t, h, r % 2, lane_place(r)).start()
+
+    def gather_end(r):
+        wait_all(abuf, 4, g2f_recv.at[r])
 
     def back(slots, carry):
         for s in slots:
@@ -479,7 +477,7 @@
     def copy_z(dz):
         return pltpu.make_async_remote_copy(
             src_ref=mis_pair, dst_ref=mis_freq.at[dz - 1],
-            send_sem=z_send.at[dz - 1], recv_sem=z_recv.at[dz - 1],
+            send_sem=z_send.at[0], recv_sem=z_recv.at[0],
             device_id={"freq": (z + dz) % freq_devices}, device_id_type=MESH,
         )
 
@@ -491,13 +489,18 @@
     def misfit_sums():
         swap_mis.wait_recv()
         mis_pair[...] = mis_own[...] + mis_other[...]
+
+        @pl.when(z < freq_devices - 1)
+        def _():
+            pl.semaphore_wait(z_here, freq_devices - 1 - z)
+
         for dz in range(1, freq_devices):
             copy_z(dz).start()
 
     def misfit_end():
+        wait_all(mis_freq, freq_devices - 1, z_recv.at[0])
         mine = mis_pair[...]
         for dz in range(1, freq_devices):
-            copy_z(dz).wait_recv()
             mine = mine + mis_freq[dz - 1]
         from_observed = lane_sum(energy[...])[:1]
         picked = jnp.zeros((mine.shape[0], part_rows), f32)
@@ -508,27 +511,6 @@
             row = row + from_observed[:, s * part_rows : (s + 1) * part_rows]
             misfit_out[pl.ds(s, 1), :] = row * f32(1.0 / (2.0 * block * lags * freq_total))
 
-    def leave1(n, carry):
-        copy1(n).wait_send()
-        return carry
-
-    def leave2(v, carry):
-        t, h, d = v // 4, (v // 2) % 2, v % 2
-        copy_a(t, h, d).wait_send()
-        for k in range(2):
-            copy_b(t, h, d, k).wait_send()
-        copy_g1(t, h, d).wait_send()
-        return carry
-
-    def leave3(v, carry):
-        t, h, d = v // 4, (v // 2) % 2, v % 2
-        copy_g1f(t, h, d).wait_send()
-        for r in range(4):
-            copy_g2(t, h, d, r).wait_send()
-        for j in range(2):
-            copy_g2f(t, h, d, j).wait_send()
-        return carry
-
     lax.fori_loop(0, 12, first_ring, 0)
     swap_ohat.start()
     energies()
@@ -547,14 +529,14 @@
         ([(gather_2, 0), (gather_lane, 0, 1)], (0, 0), (1, 2), (1, 0)),
         ([(gather_lane, 0, 3)], (0, 0), (1, 2), (3, 0)),
         ([(gather_2, 1), (misfit_parts,)], (0, 1), (0, 0), (2, 0)),
-        ([(gather_end, 0, 0), (gather_end, 1, 0)], (0, 1), (2, 0), (0, 0)),
+        ([(gather_end, 0)], (0, 1), (2, 0), (0, 0)),
         ([(gather_lane, 1, 1), (misfit_sums,)], (1, 0), (1, 2), (1, 0)),
         ([(gather_lane, 1, 3)], (1, 0), (1, 2), (3, 0)),
         ([(gather_lane, 0, 2)], (0, 0), (1, 2), (2, 0)),
         ([(gather_lane, 1, 2), (misfit_end,)], (1, 0), (1, 2), (2, 0)),
-        ([(gather_end, 0, 1), (gather_end, 1, 1)], (0, 1), (2, 0), (1, 0)),
-        ([(gather_end, 0, 3), (gather_end, 1, 3)], (0, 1), (2, 0), (3, 0)),
-        ([(gather_end, 0, 2), (gather_end, 1, 2)], (0, 1), (2, 0), (2, 0)),
+        ([(gather_end, 1)], (0, 1), (2, 0), (1, 0)),
+        ([(gather_end, 3)], (0, 1), (2, 0), (3, 0)),
+        ([(gather_end, 2)], (0, 1), (2, 0), (2, 0)),
     ]
 
     def choose(i, values):
@@ -592,16 +574,20 @@
     )
 
     swap_psd.wait_send()
-    for n in range(4):
-        swap_green(n).wait_send()
+    wait_all(gbuf.at[:, :, :, other_points], 2, green_send.at[0])
     swap_ohat.wait_send()
     swap_mis.wait_send()
     swap_sum.wait_send()
-    for dz in range(1, freq_devices):
-        copy_z(dz).wait_send()
-    lax.fori_loop(0, 48, leave1, 0)
-    lax.fori_loop(0, 8, leave2, 0)
-    lax.fori_loop(0, 8, leave3, 0)
+    wait_all(mis_freq, freq_devices - 1, z_send.at[0])
+    wait_all(send1, 24 * stages, one_send.at[0])
+    wait_all(send_a, 4 * stages, a_send.at[0])
+    wait_all(send_b, 4 * stages, b_send.at[0])
+    wait_all(abuf, 30 * stages, g_send.at[0])
+
+
+def hand_on(gradient, misfit, gradient_out, misfit_out):
+    gradient_out[...] = gradient[...]
+    misfit_out[...] = misfit[...]
 
 
 def local(green_spectra, source_psd, pair_list, owner_map, observed):
@@ -661,24 +647,22 @@
             dma((8,)),
             dma((6,)),
             dma((6,)),
+            dma((1,)),
             dma((4,)),
+            dma((1,)),
+            dma((6 * stages,)),
+            dma((1,)),
+            dma((stages,)),
+            dma((1,)),
+            dma((stages,)),
+            dma((1,)),
+            dma((stages,)),
+            dma((stages,)),
+            dma((4 * stages,)),
             dma((4,)),
-            dma((24 * stages,)),
-            dma((24 * stages,)),
-            dma((units,)),
-            dma((units,)),
-            dma((2 * units,)),
-            dma((2 * units,)),
-            dma((units,)),
-            dma((units,)),
-            dma((units,)),
-            dma((units,)),
-            dma((4 * units,)),
-            dma((4 * units,)),
-            dma((2 * units,)),
-            dma((2 * units,)),
-            dma((freq_devices - 1,)),
-            dma((freq_devices - 1,)),
+            dma((1,)),
+            dma((1,)),
+            pltpu.SemaphoreType.REGULAR,
         ],
         compiler_params=pltpu.CompilerParams(
             collective_id=0, has_side_effects=True, vmem_limit_bytes=60 * 1024 * 1024
@@ -697,7 +681,16 @@
         green_spectra.reshape(planes, freq_dev, blocks, block, points),
         observed,
     )
-    return (gradient, misfit)
+    return pl.pallas_call(
+        hand_on,
+        out_shape=(
+            jax.ShapeDtypeStruct(gradient.shape, f32),
+            jax.ShapeDtypeStruct(misfit.shape, f32),
+        ),
+        in_specs=[vmem, vmem],
+        out_specs=(vmem, vmem),
+        name="hand_on",
+    )(gradient, misfit)
 
 
 def solution(mesh):

time: 70.4 us -> 65.7 us (0.933)
  local copies, waits for them, and re-layouts: 2.46 us -> 0 us
  Pallas kernels: 67.2 us -> 64.9 us
    pallas_call x1, Pallas kernels: 67.2 us -> 63.6 us  [local(): pl.pallas_call(functools.partial(kernel, freq_devices), out_shape=(jax.Sh...]
    unnamed x2 -> x0, local copies, waits for them, and re-layouts: 2.46 us -> none
    pallas_call x0 -> x1, Pallas kernels: none -> 1.26 us  [local(): pl.pallas_call(hand_on, out_shape=(jax.ShapeDtypeStruct(gradient.shape, f...]
where the time goes in v3:
time: 65.7 us; the launch traced here: 65.5 us
  Pallas kernels  64.9 us (99%)
    pallas_call x1, Pallas kernels, local(): pl.pallas_call(functools.partial(kernel, freq_devices), out_shape=(jax.Sh...  63.6 us

profile of v3, /device:TPU:1, one launch (start us, length us, event | category | flops | bytes accessed | tf_op | source)
XLA Modules:
  0.0 65.5 jit_solution(8726680296188154744)
XLA Ops:
  0.6 63.6 %misfit_gradient.1 = (f32[2,256]{1,0:T(2,128)}, f32[2,32]{1,0:T(2,128)}) custom-call(s32[1,64]{1,0:T(1,128)} %bitcast.5, s32[2,64]{1,0:T(2,128)} %bitcast.4, f32[2,256]{1,0:T(2,128)} %psd_hbm.1, bf16[8,96,128]{2,1,0:T(8,128)(2,1)} %constant.2.clone.table, bf16[2,2,16,128,256]{4,3,2,1,0:T(8,128)(2,1)} %bitcast.3, bf16[2,128,128,128]{3,2,1,0:T(8,128)(2,1)} %observed.1), custom_call_target="tpu_custom_call" | custom-call | flops 8589934592 | bytes 12582912 | tf_op jit(solution)/shard_map/misfit_gradient/pallas_call | solution.py:607
  64.3 1.3 %hand_on.1 = (f32[2,256]{1,0:T(2,128)}, f32[2,32]{1,0:T(2,128)}) custom-call(f32[2,256]{1,0:T(2,128)} %get-tuple-element.4.gradient, f32[2,32]{1,0:T(2,128)} %get-tuple-element.5.misfit), custom_call_target="tpu_custom_call" | custom-call | tf_op jit(solution)/shard_map/hand_on/pallas_call | solution.py:684

commit v4 on v3

--- a/solution.py
+++ b/solution.py
@@ -264,15 +264,34 @@
     def wait1(i):
         wait_all(recv1, 4, one_recv.at[i])
 
+    def choose(i, values):
+        chosen = values[0]
+        for n in range(1, len(values)):
+            chosen = jnp.where(i >= n, values[n], chosen) if values[n] != values[n - 1] else chosen
+        return chosen
+
+    groups = [
+        (0, 1, 1), (0, 0, 0), (0, 0, 1), (2, 1, 0), (0, 1, 0), (2, 1, 1),
+        (1, 0, 1), (1, 0, 0), (2, 0, 1), (2, 0, 0), (1, 1, 0), (1, 1, 1),
+    ]
+
     def first_ring(i, carry):
-        part, t, j = i // 4, (i % 4) // 2, i % 2
+        part, t, j = (choose(i, [values[k] for values in groups]) for k in range(3))
         through = part == 1
         role = jnp.where(through, 2, part // 2)
         first = t * 24 + role * 8 + j * 4
 
+        @pl.when(i == 6)
+        def _():
+            load_obs.wait()
+            energies()
+
+        @pl.when((i == 6) | (i > 9))
+        def _():
+            project(jnp.where(i == 6, 0, i - 9))
+
         @pl.when(through)
         def _():
-            project(i - 4)
             wait1(t * 2 + j)
 
         slots = []
@@ -316,11 +335,13 @@
             send_b.at[i, k], recv_b.at[i, k], b_send.at[0], b_recv.at[t], neighbour(1 - h, d)
         )
 
-    def second_ring_open(t, carry):
+    def second_ring_far(t):
         for h, values in enumerate(line_sums(t, [(0, 2), (1, 2)])):
             for d in range(2):
                 send_a[place(t, h, d)] = values[d].astype(bf16)
                 copy_a(t, h, d).start()
+
+    def second_ring_near(t):
         wanted = [(h, 1 + 2 * d) for d in range(2) for h in range(2)]
         for (h, r), values in zip(wanted, line_sums(t, wanted)):
             d = r // 2
@@ -328,22 +349,19 @@
             send_b[i, 1 - d] = values[1 - d].astype(bf16)
             copy_b(t, h, d, 1 - d).start()
             keep[i] = values[d]
-        return carry
-
-    def own_part(t, carry):
+
+    def own_part(t):
         for h, values in enumerate(line_sums(t, [(0, 0), (1, 0)])):
             for k in range(2):
                 own_sum[t * 2 + h, k] = values[k]
-        return carry
-
-    def second_ring_close(t, carry):
+
+    def second_ring_close(t):
         wait_all(recv_a, 4, a_recv.at[t])
         for d in range(2):
             for h in range(2):
                 i = place(t, h, d)
                 send_b[i, d] = (keep[i] + recv_a[i].astype(f32)).astype(bf16)
                 copy_b(t, h, d, d).start()
-        return carry
 
     def copy_g1(t, h, d):
         s = slot_of(t, h, 0, 0)
@@ -430,10 +448,6 @@
         return carry
 
     def project(quarter):
-        @pl.when(quarter == 0)
-        def _():
-            load_obs.wait()
-
         chunks = block // group // 4
 
         def body(i, carry):
@@ -512,38 +526,37 @@
             misfit_out[pl.ds(s, 1), :] = row * f32(1.0 / (2.0 * block * lags * freq_total))
 
     lax.fori_loop(0, 12, first_ring, 0)
+    project(3)
     swap_ohat.start()
-    energies()
-    lax.fori_loop(0, 2, second_ring_open, 0)
-    lax.fori_loop(0, 2, own_part, 0)
-    lax.fori_loop(0, 2, second_ring_close, 0)
+    own_part(0)
+    second_ring_far(0)
+    second_ring_near(0)
+    second_ring_far(1)
+    second_ring_close(0)
+    second_ring_near(1)
+    own_part(1)
+    second_ring_close(1)
     swap_ohat.wait_recv()
     lax.fori_loop(0, 2, own_adjoint, 0)
 
     steps = [
         ([], (0, 1), (0, 0), (0, 0)),
-        ([(gather_1, 0)], (0, 0), (0, 0), (1, 2)),
-        ([(gather_lane, 0, 0)], (0, 0), (1, 2), (0, 0)),
+        ([(misfit_parts,), (gather_1, 0)], (0, 0), (0, 0), (1, 2)),
         ([(gather_1, 1)], (1, 0), (0, 0), (1, 2)),
+        ([(gather_lane, 0, 0), (misfit_sums,)], (0, 0), (1, 2), (0, 0)),
         ([(gather_lane, 1, 0)], (1, 0), (1, 2), (0, 0)),
-        ([(gather_2, 0), (gather_lane, 0, 1)], (0, 0), (1, 2), (1, 0)),
-        ([(gather_lane, 0, 3)], (0, 0), (1, 2), (3, 0)),
-        ([(gather_2, 1), (misfit_parts,)], (0, 1), (0, 0), (2, 0)),
+        ([(gather_lane, 0, 1)], (0, 0), (1, 2), (1, 0)),
+        ([(gather_2, 0), (gather_lane, 0, 3)], (0, 0), (1, 2), (3, 0)),
+        ([(gather_2, 1)], (0, 1), (0, 0), (2, 0)),
+        ([(gather_lane, 1, 1)], (1, 0), (1, 2), (1, 0)),
+        ([(gather_lane, 1, 3)], (1, 0), (1, 2), (3, 0)),
         ([(gather_end, 0)], (0, 1), (2, 0), (0, 0)),
-        ([(gather_lane, 1, 1), (misfit_sums,)], (1, 0), (1, 2), (1, 0)),
-        ([(gather_lane, 1, 3)], (1, 0), (1, 2), (3, 0)),
         ([(gather_lane, 0, 2)], (0, 0), (1, 2), (2, 0)),
-        ([(gather_lane, 1, 2), (misfit_end,)], (1, 0), (1, 2), (2, 0)),
+        ([(gather_lane, 1, 2)], (1, 0), (1, 2), (2, 0)),
         ([(gather_end, 1)], (0, 1), (2, 0), (1, 0)),
         ([(gather_end, 3)], (0, 1), (2, 0), (3, 0)),
         ([(gather_end, 2)], (0, 1), (2, 0), (2, 0)),
     ]
-
-    def choose(i, values):
-        chosen = values[0]
-        for n in range(1, len(values)):
-            chosen = jnp.where(i >= n, values[n], chosen) if values[n] != values[n - 1] else chosen
-        return chosen
 
     def gather_step(i, carry):
         for n, step in enumerate(steps):
@@ -567,6 +580,7 @@
     gsend[...] = jnp.broadcast_to(lines[:, points:], gsend.shape)
     swap_sum = remote(gsend, grecv, core_send.at[5], core_recv.at[5], other)
     swap_sum.start()
+    misfit_end()
     swap_sum.wait_recv()
     row_ids = lax.broadcasted_iota(jnp.int32, (2, points), 0)
     gradient_out[...] = jnp.where(

time: 65.7 us -> 64 us (0.974)
  Pallas kernels: 64.9 us -> 63.3 us
    pallas_call x1, Pallas kernels: 63.6 us -> 62 us  [local(): pl.pallas_call(functools.partial(kernel, freq_devices), out_shape=(jax.Sh...]
where the time goes in v4:
time: 64 us; the launch traced here: 63.9 us
  Pallas kernels  63.3 us (99%)
  between operations  0.64 us (1%)
    pallas_call x1, Pallas kernels, local(): pl.pallas_call(functools.partial(kernel, freq_devices), out_shape=(jax.Sh...  62 us

profile of v4, /device:TPU:1, one launch (start us, length us, event | category | flops | bytes accessed | tf_op | source)
XLA Modules:
  0.0 63.9 jit_solution(1360941160203237286)
XLA Ops:
  0.6 62.0 %misfit_gradient.1 = (f32[2,256]{1,0:T(2,128)}, f32[2,32]{1,0:T(2,128)}) custom-call(s32[1,64]{1,0:T(1,128)} %bitcast.5, s32[2,64]{1,0:T(2,128)} %bitcast.4, f32[2,256]{1,0:T(2,128)} %psd_hbm.1, bf16[8,96,128]{2,1,0:T(8,128)(2,1)} %constant.2.clone.table, bf16[2,2,16,128,256]{4,3,2,1,0:T(8,128)(2,1)} %bitcast.3, bf16[2,128,128,128]{3,2,1,0:T(8,128)(2,1)} %observed.1), custom_call_target="tpu_custom_call" | custom-call | flops 8589934592 | bytes 12582912 | tf_op jit(solution)/shard_map/misfit_gradient/pallas_call | solution.py:621
  62.6 1.3 %hand_on.1 = (f32[2,256]{1,0:T(2,128)}, f32[2,32]{1,0:T(2,128)}) custom-call(f32[2,256]{1,0:T(2,128)} %get-tuple-element.4.gradient, f32[2,32]{1,0:T(2,128)} %get-tuple-element.5.misfit), custom_call_target="tpu_custom_call" | custom-call | tf_op jit(solution)/shard_map/hand_on/pallas_call | solution.py:698

commit v5 on v4

--- a/solution.py
+++ b/solution.py
@@ -96,6 +96,7 @@
     z_send,
     z_recv,
     z_here,
+    near_here,
 ):
     z = lax.axis_index("freq")
     g = lax.axis_index("grid")
@@ -133,18 +134,30 @@
         )
 
     barrier = pltpu.get_barrier_semaphore()
-    friends = [{"grid": other}]
-    for axis in range(2):
-        for d in range(2):
-            friends.append({"grid": neighbour(axis, d)})
-    for friend in friends:
-        pl.semaphore_signal(barrier, inc=1, device_id=friend, device_id_type=MESH)
+    def distance(p):
+        return jnp.minimum(p, side - p)
+
+    lower = distance(x) + distance(y)
+    pl.semaphore_signal(barrier, inc=1, device_id={"grid": other}, device_id_type=MESH)
+
+    def greet(semaphore, upward):
+        for axis, p in enumerate((x, y)):
+            for d in range(2):
+                q = (p + 1 + 2 * d) % side
+                near, far = (distance(p), distance(q)) if upward else (distance(q), distance(p))
+
+                @pl.when(near < far)
+                def _():
+                    pl.semaphore_signal(
+                        semaphore, inc=1, device_id={"grid": neighbour(axis, d)}, device_id_type=MESH
+                    )
+
+    greet(barrier, True)
     for dz in range(1, freq_devices):
 
         @pl.when(z + dz < freq_devices)
         def _():
             pl.semaphore_signal(barrier, inc=1, device_id={"freq": z + dz}, device_id_type=MESH)
-
 
     own_points = pl.ds(0, points)
     other_points = pl.ds(points, points)
@@ -163,13 +176,7 @@
     for copy in load_green:
         copy.start()
     load_table.start()
-    pl.semaphore_wait(barrier, len(friends) + z)
-    for dz in range(1, freq_devices):
-
-        @pl.when(z >= dz)
-        def _():
-            pl.semaphore_signal(z_here, inc=1, device_id={"freq": z - dz}, device_id_type=MESH)
-
+    pl.semaphore_wait(barrier, 1 + lower + z)
 
     swap_psd = remote(psd_hbm, psd_other, core_send.at[2], core_recv.at[2], other)
     half = gbuf.shape[1] // 2
@@ -185,6 +192,13 @@
     for n in range(4):
         swap_green(n).start()
     load_obs.start()
+
+    greet(near_here, False)
+    for dz in range(1, freq_devices):
+
+        @pl.when(z >= dz)
+        def _():
+            pl.semaphore_signal(z_here, inc=1, device_id={"freq": z - dz}, device_id_type=MESH)
 
     def weigh(k, first, count, where, row):
         def body(b, carry):
@@ -305,6 +319,10 @@
             with_n = jnp.where(through, n - 16, 48)
             for k in range(2):
                 send1[n, k] = (values[k] + recv1[with_n, k].astype(f32)).astype(bf16)
+        @pl.when((i == 0) & (lower < side))
+        def _():
+            pl.semaphore_wait(near_here, side - lower)
+
         for u in range(4):
             copy1(first + u).start()
         return carry
@@ -434,17 +452,17 @@
     def gather_end(r):
         wait_all(abuf, 4, g2f_recv.at[r])
 
-    def back(slots, carry):
+    def back(slots, carry, where, count):
         for s in slots:
             weights = abuf[s]
             top = jnp.concatenate((weights[0], -weights[1]), axis=1)
             low = jnp.concatenate((weights[1], weights[0]), axis=1)
-            right = gbuf[:, ids[1, s]].reshape(2 * block, 2 * points)
+            right = gbuf[:, ids[1, s], :, where].reshape(2 * block, count)
             moved = jnp.dot(
                 jnp.concatenate((top, low), axis=0), right, preferred_element_type=f32
             )
-            left = gbuf[:, ids[0, s]].reshape(2 * block, 2 * points).astype(f32)
-            carry = carry + jnp.sum((moved * left).reshape(2 * block // 8, 8, 2 * points), axis=0)
+            left = gbuf[:, ids[0, s], :, where].reshape(2 * block, count).astype(f32)
+            carry = carry + jnp.sum((moved * left).reshape(2 * block // 8, 8, count), axis=0)
         return carry
 
     def project(quarter):
@@ -555,7 +573,6 @@
         ([(gather_lane, 1, 2)], (1, 0), (1, 2), (2, 0)),
         ([(gather_end, 1)], (0, 1), (2, 0), (1, 0)),
         ([(gather_end, 3)], (0, 1), (2, 0), (3, 0)),
-        ([(gather_end, 2)], (0, 1), (2, 0), (2, 0)),
     ]
 
     def gather_step(i, carry):
@@ -572,19 +589,27 @@
                 choose(i, [step[part][0] + u // 2 * step[part][1] for step in steps]) for part in (1, 2, 3)
             )
             slots.append(slot_of(t, u % 2, o, r))
-        return back(slots, carry)
+        return back(slots, carry, pl.ds(0, 2 * points), 2 * points)
 
     gsum[...] = lax.fori_loop(0, len(steps), gather_step, gsum[...])
 
-    lines = jnp.sum(gsum[...], axis=0, keepdims=True) * f32(1.0 / (block * math.sqrt(slot_count)))
-    gsend[...] = jnp.broadcast_to(lines[:, points:], gsend.shape)
+    gather_end(2)
+    last = [slot_of(t, h, 2, 2) for t in range(stages) for h in range(2)]
+    scale = f32(1.0 / (block * math.sqrt(slot_count)))
+
+    def finish(where):
+        parts = back(last, gsum[:, where], where, points)
+        return jnp.sum(parts, axis=0, keepdims=True) * scale
+
+    gsend[...] = jnp.broadcast_to(finish(other_points), gsend.shape)
     swap_sum = remote(gsend, grecv, core_send.at[5], core_recv.at[5], other)
     swap_sum.start()
+    own_lines = finish(own_points)
     misfit_end()
+    row_ids = lax.broadcasted_iota(jnp.int32, (2, points), 0)
     swap_sum.wait_recv()
-    row_ids = lax.broadcasted_iota(jnp.int32, (2, points), 0)
     gradient_out[...] = jnp.where(
-        row_ids == c, jnp.broadcast_to(lines[:, :points], (2, points)), grecv[:2]
+        row_ids == c, jnp.broadcast_to(own_lines, (2, points)), grecv[:2]
     )
 
     swap_psd.wait_send()
@@ -677,6 +702,7 @@
             dma((1,)),
             dma((1,)),
             pltpu.SemaphoreType.REGULAR,
+            pltpu.SemaphoreType.REGULAR,
         ],
         compiler_params=pltpu.CompilerParams(
             collective_id=0, has_side_effects=True, vmem_limit_bytes=60 * 1024 * 1024

time: 64 us -> 63.1 us (0.986)
  Pallas kernels: 63.3 us -> 62.3 us
    pallas_call x1, Pallas kernels: 62 us -> 61 us  [local(): pl.pallas_call(functools.partial(kernel, freq_devices), out_shape=(jax.Sh...]
where the time goes in v5:
time: 63.1 us; the launch traced here: 62.9 us
  Pallas kernels  62.3 us (99%)
  between operations  0.64 us (1%)
    pallas_call x1, Pallas kernels, local(): pl.pallas_call(functools.partial(kernel, freq_devices), out_shape=(jax.Sh...  61 us

profile of v5, /device:TPU:1, one launch (start us, length us, event | category | flops | bytes accessed | tf_op | source)
XLA Modules:
  0.0 62.9 jit_solution(9630039064128309664)
XLA Ops:
  0.6 61.0 %misfit_gradient.1 = (f32[2,256]{1,0:T(2,128)}, f32[2,32]{1,0:T(2,128)}) custom-call(s32[1,64]{1,0:T(1,128)} %bitcast.5, s32[2,64]{1,0:T(2,128)} %bitcast.4, f32[2,256]{1,0:T(2,128)} %psd_hbm.1, bf16[8,96,128]{2,1,0:T(8,128)(2,1)} %constant.2.clone.table, bf16[2,2,16,128,256]{4,3,2,1,0:T(8,128)(2,1)} %bitcast.3, bf16[2,128,128,128]{3,2,1,0:T(8,128)(2,1)} %observed.1), custom_call_target="tpu_custom_call" | custom-call | flops 8589934592 | bytes 12582912 | tf_op jit(solution)/shard_map/misfit_gradient/pallas_call | solution.py:646
  61.7 1.3 %hand_on.1 = (f32[2,256]{1,0:T(2,128)}, f32[2,32]{1,0:T(2,128)}) custom-call(f32[2,256]{1,0:T(2,128)} %get-tuple-element.4.gradient, f32[2,32]{1,0:T(2,128)} %get-tuple-element.5.misfit), custom_call_target="tpu_custom_call" | custom-call | tf_op jit(solution)/shard_map/hand_on/pallas_call | solution.py:724

commit v6 on v5

--- a/solution.py
+++ b/solution.py
@@ -46,8 +46,13 @@
     observed,
     gradient_out,
     misfit_out,
-    gbuf,
-    wbuf,
+    green_own,
+    green_other,
+    green_cross,
+    weighted_own,
+    weighted_other,
+    cross_send,
+    cross_recv,
     psd,
     psd_other,
     owner_row,
@@ -133,6 +138,15 @@
             device_id={"grid": device}, device_id_type=MESH,
         )
 
+    def copy1(n):
+        t, role, u = n // 24, (n % 24) // 8, n % 8
+        h, d, j = u % 2, (u // 2) % 2, u // 4
+        r = jnp.where(role == 1, lane(1 - d, j), lane(d, j))
+        i = jnp.where(role == 0, t * 2 + j, 4 + t * 4 + r)
+        return remote(send1.at[n], recv1.at[n], one_send.at[0], one_recv.at[i], neighbour(h, d))
+
+    early_first = 24 + 4
+
     barrier = pltpu.get_barrier_semaphore()
     def distance(p):
         return jnp.minimum(p, side - p)
@@ -159,39 +173,34 @@
         def _():
             pl.semaphore_signal(barrier, inc=1, device_id={"freq": z + dz}, device_id_type=MESH)
 
-    own_points = pl.ds(0, points)
-    other_points = pl.ds(points, points)
     load_owner = pltpu.make_async_copy(owner, owner_row, local_sem.at[4])
     load_pairs = pltpu.make_async_copy(pairs, pair_rows, local_sem.at[5])
     load_psd = pltpu.make_async_copy(psd_hbm, psd, local_sem.at[6])
-    load_green = [
-        pltpu.make_async_copy(green.at[k, c], gbuf.at[k, :, :, own_points], local_sem.at[k])
-        for k in range(2)
-    ]
+    load_green = pltpu.make_async_copy(green.at[:, c], green_own, local_sem.at[0])
+    load_cross = pltpu.make_async_copy(green.at[:, 1 - c], green_cross, local_sem.at[1])
     load_table = pltpu.make_async_copy(table.at[z * 2 + c], phi, local_sem.at[2])
     load_obs = pltpu.make_async_copy(observed, obs, local_sem.at[3])
     load_owner.start()
     load_pairs.start()
     load_psd.start()
-    for copy in load_green:
-        copy.start()
+    load_cross.start()
+    load_green.start()
     load_table.start()
     pl.semaphore_wait(barrier, 1 + lower + z)
 
     swap_psd = remote(psd_hbm, psd_other, core_send.at[2], core_recv.at[2], other)
-    half = gbuf.shape[1] // 2
+    parts = 4
+    blocks = green.shape[2]
 
     def swap_green(n):
-        k, some = n // 2, pl.ds(n % 2 * half, half)
+        k, some = n // parts, pl.ds(n % parts * (blocks // parts), blocks // parts)
         return remote(
-            green.at[k, 1 - c, some], gbuf.at[k, some, :, other_points],
-            green_send.at[0], green_recv.at[n], other,
+            green.at[k, 1 - c, some], green_other.at[k, some], green_send.at[0], green_recv.at[n], other
         )
 
     swap_psd.start()
-    for n in range(4):
+    for n in range(3):
         swap_green(n).start()
-    load_obs.start()
 
     greet(near_here, False)
     for dz in range(1, freq_devices):
@@ -200,14 +209,18 @@
         def _():
             pl.semaphore_signal(z_here, inc=1, device_id={"freq": z - dz}, device_id_type=MESH)
 
-    def weigh(k, first, count, where, row):
+    def weigh(k, first, count, source, result, row):
         def body(b, carry):
             for i in range(4):
                 place = first + 4 * b + i
-                wbuf[k, place, :, where] = (gbuf[k, place, :, where].astype(f32) * row).astype(bf16)
+                result[k, place] = (source[k, place].astype(f32) * row).astype(bf16)
             return carry
 
         lax.fori_loop(0, count // 4, body, 0)
+
+    def cross_parts(left, right):
+        acc = lax.dot_general(left, right, (((1,), (1,)), ((), ())), preferred_element_type=f32)
+        return acc[:block, :block] + acc[block:, block:], acc[block:, :block] - acc[:block, block:]
 
     load_owner.wait()
     load_pairs.wait()
@@ -230,11 +243,45 @@
     move_ids = pltpu.make_async_copy(ids_row, ids, local_sem.at[7])
     move_ids.start()
 
+    early = [slot_of(1, u % 2, 2, lane(u // 2, 1)) for u in range(4)]
     load_psd.wait()
+    cross_row = psd[pl.ds(1 - c, 1), :]
+    load_cross.wait()
+    move_ids.wait()
+    for u, slot in enumerate(early):
+        left = (green_cross[:, ids[0, slot]].astype(f32) * cross_row).astype(bf16)
+        right = green_cross[:, ids[1, slot]]
+        values = cross_parts(left.reshape(2 * block, points), right.reshape(2 * block, points))
+        for k in range(2):
+            cross_send[u, k] = values[k].astype(bf16)
+    swap_cross = remote(cross_send, cross_recv, core_send.at[0], core_recv.at[0], other)
+    swap_cross.start()
+    for n in range(3, 2 * parts):
+        swap_green(n).start()
+    load_obs.start()
+
     own_row = psd[pl.ds(c, 1), :]
+    load_green.wait()
     for k in range(2):
-        load_green[k].wait()
-        weigh(k, 0, 2 * half, own_points, own_row)
+        weigh(k, 0, blocks, green_own, weighted_own, own_row)
+    early_shares = [
+        cross_parts(
+            weighted_own[:, ids[0, slot]].reshape(2 * block, points),
+            green_own[:, ids[1, slot]].reshape(2 * block, points),
+        )
+        for slot in early
+    ]
+    swap_cross.wait_recv()
+    for u, values in enumerate(early_shares):
+        for k in range(2):
+            send1[early_first + u, k] = (values[k] + cross_recv[u, k].astype(f32)).astype(bf16)
+
+    @pl.when(lower < side)
+    def _():
+        pl.semaphore_wait(near_here, side - lower)
+
+    for u in range(4):
+        copy1(early_first + u).start()
 
     load_table.wait()
     rows = phi.shape[0]
@@ -246,30 +293,23 @@
     recv1[48] = jnp.zeros_like(recv1[48])
     gsum[...] = jnp.zeros_like(gsum)
     mis_own[...] = jnp.zeros_like(mis_own)
-    move_ids.wait()
     swap_psd.wait_recv()
     other_row = psd_other[pl.ds(c, 1), :]
-    for n in range(4):
+    for n in range(2 * parts):
         swap_green(n).wait_recv()
-        weigh(n // 2, n % 2 * half, half, other_points, other_row)
+        weigh(n // parts, n % parts * (blocks // parts), blocks // parts, green_other, weighted_other, other_row)
+
+    def both(own, others, place):
+        return jnp.concatenate((own[:, place], others[:, place]), axis=2).reshape(2 * block, 2 * points)
 
     def units(slots):
-        pairs_of = []
-        for slot in slots:
-            left = wbuf[:, ids[0, slot]].reshape(2 * block, 2 * points)
-            right = gbuf[:, ids[1, slot]].reshape(2 * block, 2 * points)
-            acc = lax.dot_general(left, right, (((1,), (1,)), ((), ())), preferred_element_type=f32)
-            real = acc[:block, :block] + acc[block:, block:]
-            imag = acc[block:, :block] - acc[:block, block:]
-            pairs_of.append((real, imag))
-        return pairs_of
-
-    def copy1(n):
-        t, role, u = n // 24, (n % 24) // 8, n % 8
-        h, d, j = u % 2, (u // 2) % 2, u // 4
-        r = jnp.where(role == 1, lane(1 - d, j), lane(d, j))
-        i = jnp.where(role == 0, t * 2 + j, 4 + t * 4 + r)
-        return remote(send1.at[n], recv1.at[n], one_send.at[0], one_recv.at[i], neighbour(h, d))
+        return [
+            cross_parts(
+                both(weighted_own, weighted_other, ids[0, slot]),
+                both(green_own, green_other, ids[1, slot]),
+            )
+            for slot in slots
+        ]
 
     def wait_all(buffer, count, semaphore):
         some = buffer.at[pl.ds(0, count)]
@@ -319,10 +359,6 @@
             with_n = jnp.where(through, n - 16, 48)
             for k in range(2):
                 send1[n, k] = (values[k] + recv1[with_n, k].astype(f32)).astype(bf16)
-        @pl.when((i == 0) & (lower < side))
-        def _():
-            pl.semaphore_wait(near_here, side - lower)
-
         for u in range(4):
             copy1(first + u).start()
         return carry
@@ -452,16 +488,16 @@
     def gather_end(r):
         wait_all(abuf, 4, g2f_recv.at[r])
 
-    def back(slots, carry, where, count):
+    def back(slots, carry, of_block, count):
         for s in slots:
             weights = abuf[s]
             top = jnp.concatenate((weights[0], -weights[1]), axis=1)
             low = jnp.concatenate((weights[1], weights[0]), axis=1)
-            right = gbuf[:, ids[1, s], :, where].reshape(2 * block, count)
+            right = of_block(ids[1, s])
             moved = jnp.dot(
                 jnp.concatenate((top, low), axis=0), right, preferred_element_type=f32
             )
-            left = gbuf[:, ids[0, s], :, where].reshape(2 * block, count).astype(f32)
+            left = of_block(ids[0, s]).astype(f32)
             carry = carry + jnp.sum((moved * left).reshape(2 * block // 8, 8, count), axis=0)
         return carry
 
@@ -543,7 +579,7 @@
             row = row + from_observed[:, s * part_rows : (s + 1) * part_rows]
             misfit_out[pl.ds(s, 1), :] = row * f32(1.0 / (2.0 * block * lags * freq_total))
 
-    lax.fori_loop(0, 12, first_ring, 0)
+    lax.fori_loop(1, 12, first_ring, 0)
     project(3)
     swap_ohat.start()
     own_part(0)
@@ -589,7 +625,7 @@
                 choose(i, [step[part][0] + u // 2 * step[part][1] for step in steps]) for part in (1, 2, 3)
             )
             slots.append(slot_of(t, u % 2, o, r))
-        return back(slots, carry, pl.ds(0, 2 * points), 2 * points)
+        return back(slots, carry, lambda place: both(green_own, green_other, place), 2 * points)
 
     gsum[...] = lax.fori_loop(0, len(steps), gather_step, gsum[...])
 
@@ -597,14 +633,15 @@
     last = [slot_of(t, h, 2, 2) for t in range(stages) for h in range(2)]
     scale = f32(1.0 / (block * math.sqrt(slot_count)))
 
-    def finish(where):
-        parts = back(last, gsum[:, where], where, points)
-        return jnp.sum(parts, axis=0, keepdims=True) * scale
-
-    gsend[...] = jnp.broadcast_to(finish(other_points), gsend.shape)
+    def finish(buffer, first):
+        sums = gsum[:, first : first + points]
+        sums = back(last, sums, lambda place: buffer[:, place].reshape(2 * block, points), points)
+        return jnp.sum(sums, axis=0, keepdims=True) * scale
+
+    gsend[...] = jnp.broadcast_to(finish(green_other, points), gsend.shape)
     swap_sum = remote(gsend, grecv, core_send.at[5], core_recv.at[5], other)
     swap_sum.start()
-    own_lines = finish(own_points)
+    own_lines = finish(green_own, 0)
     misfit_end()
     row_ids = lax.broadcasted_iota(jnp.int32, (2, points), 0)
     swap_sum.wait_recv()
@@ -613,7 +650,8 @@
     )
 
     swap_psd.wait_send()
-    wait_all(gbuf.at[:, :, :, other_points], 2, green_send.at[0])
+    wait_all(green_other, 2, green_send.at[0])
+    swap_cross.wait_send()
     swap_ohat.wait_send()
     swap_mis.wait_send()
     swap_sum.wait_send()
@@ -652,8 +690,13 @@
         in_specs=[hbm] * 6,
         out_specs=(vmem, vmem),
         scratch_shapes=[
-            pltpu.VMEM((2, blocks, block, 2 * points), bf16),
-            pltpu.VMEM((2, blocks, block, 2 * points), bf16),
+            pltpu.VMEM((2, blocks, block, points), bf16),
+            pltpu.VMEM((2, blocks, block, points), bf16),
+            pltpu.VMEM((2, blocks, block, points), bf16),
+            pltpu.VMEM((2, blocks, block, points), bf16),
+            pltpu.VMEM((2, blocks, block, points), bf16),
+            pltpu.VMEM((4,) + pair, bf16),
+            pltpu.VMEM((4,) + pair, bf16),
             pltpu.VMEM((freq_dev, points), f32),
             pltpu.VMEM((freq_dev, points), f32),
             pltpu.VMEM((1, slot_count), jnp.int32),
@@ -687,7 +730,7 @@
             dma((6,)),
             dma((6,)),
             dma((1,)),
-            dma((4,)),
+            dma((8,)),
             dma((1,)),
             dma((6 * stages,)),
             dma((1,)),

time: 63.1 us -> 62.3 us (0.987)
  Pallas kernels: 62.3 us -> 61.6 us
    pallas_call x1, Pallas kernels: 61 us -> 60.3 us  [local(): pl.pallas_call(functools.partial(kernel, freq_devices), out_shape=(jax.Sh...]
where the time goes in v6:
time: 62.3 us; the launch traced here: 62.2 us
  Pallas kernels  61.6 us (99%)
  between operations  0.64 us (1%)
    pallas_call x1, Pallas kernels, local(): pl.pallas_call(functools.partial(kernel, freq_devices), out_shape=(jax.Sh...  60.3 us
    pallas_call x1, Pallas kernels, local(): pl.pallas_call(hand_on, out_shape=(jax.ShapeDtypeStruct(gradient.shape, f...  1.26 us

profile of v6, /device:TPU:1, one launch (start us, length us, event | category | flops | bytes accessed | tf_op | source)
XLA Modules:
  0.0 62.2 jit_solution(9402298757184859475)
XLA Ops:
  0.6 60.3 %misfit_gradient.1 = (f32[2,256]{1,0:T(2,128)}, f32[2,32]{1,0:T(2,128)}) custom-call(s32[1,64]{1,0:T(1,128)} %bitcast.5, s32[2,64]{1,0:T(2,128)} %bitcast.4, f32[2,256]{1,0:T(2,128)} %psd_hbm.1, bf16[8,96,128]{2,1,0:T(8,128)(2,1)} %constant.2.clone.table, bf16[2,2,16,128,256]{4,3,2,1,0:T(8,128)(2,1)} %bitcast.3, bf16[2,128,128,128]{3,2,1,0:T(8,128)(2,1)} %observed.1), custom_call_target="tpu_custom_call" | custom-call | flops 8589934592 | bytes 12582912 | tf_op jit(solution)/shard_map/misfit_gradient/pallas_call | solution.py:684
  60.9 1.3 %hand_on.1 = (f32[2,256]{1,0:T(2,128)}, f32[2,32]{1,0:T(2,128)}) custom-call(f32[2,256]{1,0:T(2,128)} %get-tuple-element.4.gradient, f32[2,32]{1,0:T(2,128)} %get-tuple-element.5.misfit), custom_call_target="tpu_custom_call" | custom-call | tf_op jit(solution)/shard_map/hand_on/pallas_call | solution.py:767

commit v7 on v6

--- a/solution.py
+++ b/solution.py
@@ -145,7 +145,7 @@
         i = jnp.where(role == 0, t * 2 + j, 4 + t * 4 + r)
         return remote(send1.at[n], recv1.at[n], one_send.at[0], one_recv.at[i], neighbour(h, d))
 
-    early_first = 24 + 4
+    early = [(1, 1), (0, 0)]
 
     barrier = pltpu.get_barrier_semaphore()
     def distance(p):
@@ -243,20 +243,30 @@
     move_ids = pltpu.make_async_copy(ids_row, ids, local_sem.at[7])
     move_ids.start()
 
-    early = [slot_of(1, u % 2, 2, lane(u // 2, 1)) for u in range(4)]
+    def early_slots(t, j):
+        return [slot_of(t, u % 2, 2, lane(u // 2, j)) for u in range(4)]
+
+    def swap_cross(e):
+        some = pl.ds(4 * e, 4)
+        return remote(
+            cross_send.at[some], cross_recv.at[some], core_send.at[e], core_recv.at[e], other
+        )
+
     load_psd.wait()
     cross_row = psd[pl.ds(1 - c, 1), :]
     load_cross.wait()
     move_ids.wait()
-    for u, slot in enumerate(early):
-        left = (green_cross[:, ids[0, slot]].astype(f32) * cross_row).astype(bf16)
-        right = green_cross[:, ids[1, slot]]
-        values = cross_parts(left.reshape(2 * block, points), right.reshape(2 * block, points))
-        for k in range(2):
-            cross_send[u, k] = values[k].astype(bf16)
-    swap_cross = remote(cross_send, cross_recv, core_send.at[0], core_recv.at[0], other)
-    swap_cross.start()
-    for n in range(3, 2 * parts):
+    for e, (t, j) in enumerate(early):
+        for u, slot in enumerate(early_slots(t, j)):
+            left = (green_cross[:, ids[0, slot]].astype(f32) * cross_row).astype(bf16)
+            right = green_cross[:, ids[1, slot]]
+            values = cross_parts(left.reshape(2 * block, points), right.reshape(2 * block, points))
+            for k in range(2):
+                cross_send[4 * e + u, k] = values[k].astype(bf16)
+        swap_cross(e).start()
+        if e == 0:
+            swap_green(3).start()
+    for n in range(4, 2 * parts):
         swap_green(n).start()
     load_obs.start()
 
@@ -264,24 +274,27 @@
     load_green.wait()
     for k in range(2):
         weigh(k, 0, blocks, green_own, weighted_own, own_row)
-    early_shares = [
-        cross_parts(
-            weighted_own[:, ids[0, slot]].reshape(2 * block, points),
-            green_own[:, ids[1, slot]].reshape(2 * block, points),
-        )
-        for slot in early
-    ]
-    swap_cross.wait_recv()
-    for u, values in enumerate(early_shares):
-        for k in range(2):
-            send1[early_first + u, k] = (values[k] + cross_recv[u, k].astype(f32)).astype(bf16)
-
-    @pl.when(lower < side)
-    def _():
-        pl.semaphore_wait(near_here, side - lower)
-
-    for u in range(4):
-        copy1(early_first + u).start()
+    for e, (t, j) in enumerate(early):
+        shares = [
+            cross_parts(
+                weighted_own[:, ids[0, slot]].reshape(2 * block, points),
+                green_own[:, ids[1, slot]].reshape(2 * block, points),
+            )
+            for slot in early_slots(t, j)
+        ]
+        swap_cross(e).wait_recv()
+        first = t * 24 + j * 4
+        for u, values in enumerate(shares):
+            for k in range(2):
+                send1[first + u, k] = (values[k] + cross_recv[4 * e + u, k].astype(f32)).astype(bf16)
+        if e == 0:
+
+            @pl.when(lower < side)
+            def _():
+                pl.semaphore_wait(near_here, side - lower)
+
+        for u in range(4):
+            copy1(first + u).start()
 
     load_table.wait()
     rows = phi.shape[0]
@@ -325,8 +338,8 @@
         return chosen
 
     groups = [
-        (0, 1, 1), (0, 0, 0), (0, 0, 1), (2, 1, 0), (0, 1, 0), (2, 1, 1),
-        (1, 0, 1), (1, 0, 0), (2, 0, 1), (2, 0, 0), (1, 1, 0), (1, 1, 1),
+        (0, 1, 1), (0, 0, 0), (0, 0, 1), (0, 1, 0), (2, 0, 0), (2, 0, 1),
+        (1, 0, 0), (1, 0, 1), (2, 1, 0), (2, 1, 1), (1, 1, 0), (1, 1, 1),
     ]
 
     def first_ring(i, carry):
@@ -340,9 +353,9 @@
             load_obs.wait()
             energies()
 
-        @pl.when((i == 6) | (i > 9))
+        @pl.when((i == 6) | (i == 8) | (i == 10))
         def _():
-            project(jnp.where(i == 6, 0, i - 9))
+            project(jnp.where(i == 6, 0, jnp.where(i == 8, 1, 2)))
 
         @pl.when(through)
         def _():
@@ -579,7 +592,7 @@
             row = row + from_observed[:, s * part_rows : (s + 1) * part_rows]
             misfit_out[pl.ds(s, 1), :] = row * f32(1.0 / (2.0 * block * lags * freq_total))
 
-    lax.fori_loop(1, 12, first_ring, 0)
+    lax.fori_loop(len(early), 12, first_ring, 0)
     project(3)
     swap_ohat.start()
     own_part(0)
@@ -651,7 +664,8 @@
 
     swap_psd.wait_send()
     wait_all(green_other, 2, green_send.at[0])
-    swap_cross.wait_send()
+    for e in range(len(early)):
+        swap_cross(e).wait_send()
     swap_ohat.wait_send()
     swap_mis.wait_send()
     swap_sum.wait_send()
@@ -695,8 +709,8 @@
             pltpu.VMEM((2, blocks, block, points), bf16),
             pltpu.VMEM((2, blocks, block, points), bf16),
             pltpu.VMEM((2, blocks, block, points), bf16),
-            pltpu.VMEM((4,) + pair, bf16),
-            pltpu.VMEM((4,) + pair, bf16),
+            pltpu.VMEM((8,) + pair, bf16),
+            pltpu.VMEM((8,) + pair, bf16),
             pltpu.VMEM((freq_dev, points), f32),
             pltpu.VMEM((freq_dev, points), f32),
             pltpu.VMEM((1, slot_count), jnp.int32),

time: 62.3 us -> 61.2 us (0.982)
  Pallas kernels: 61.6 us -> 60.4 us
    pallas_call x1, Pallas kernels: 60.3 us -> 59.2 us  [local(): pl.pallas_call(functools.partial(kernel, freq_devices), out_shape=(jax.Sh...]
where the time goes in v7:
time: 61.2 us; the launch traced here: 61.1 us
  Pallas kernels  60.4 us (99%)
  between operations  0.64 us (1%)
    pallas_call x1, Pallas kernels, local(): pl.pallas_call(functools.partial(kernel, freq_devices), out_shape=(jax.Sh...  59.2 us
    pallas_call x1, Pallas kernels, local(): pl.pallas_call(hand_on, out_shape=(jax.ShapeDtypeStruct(gradient.shape, f...  1.26 us

profile of v7, /device:TPU:1, one launch (start us, length us, event | category | flops | bytes accessed | tf_op | source)
XLA Modules:
  0.0 61.1 jit_solution(8886728811685866039)
XLA Ops:
  0.6 59.2 %misfit_gradient.1 = (f32[2,256]{1,0:T(2,128)}, f32[2,32]{1,0:T(2,128)}) custom-call(s32[1,64]{1,0:T(1,128)} %bitcast.5, s32[2,64]{1,0:T(2,128)} %bitcast.4, f32[2,256]{1,0:T(2,128)} %psd_hbm.1, bf16[8,96,128]{2,1,0:T(8,128)(2,1)} %constant.2.clone.table, bf16[2,2,16,128,256]{4,3,2,1,0:T(8,128)(2,1)} %bitcast.3, bf16[2,128,128,128]{3,2,1,0:T(8,128)(2,1)} %observed.1), custom_call_target="tpu_custom_call" | custom-call | flops 8589934592 | bytes 12582912 | tf_op jit(solution)/shard_map/misfit_gradient/pallas_call | solution.py:698
  59.8 1.3 %hand_on.1 = (f32[2,256]{1,0:T(2,128)}, f32[2,32]{1,0:T(2,128)}) custom-call(f32[2,256]{1,0:T(2,128)} %get-tuple-element.4.gradient, f32[2,32]{1,0:T(2,128)} %get-tuple-element.5.misfit), custom_call_target="tpu_custom_call" | custom-call | tf_op jit(solution)/shard_map/hand_on/pallas_call | solution.py:781

commit v8 on v7

--- a/solution.py
+++ b/solution.py
@@ -470,22 +470,22 @@
                 kept = kept + cross * (f32(lags / 2) * cross - 2.0 * seen)
             for d in range(2):
                 copy_g1(t, h, d).start()
+            total[q] = kept
+        for h in range(2):
             for d in range(2):
                 copy_g2(t, h, d, 0).start()
-            total[q] = kept
         return carry
 
     def gather_1(t):
         wait_all(abuf, 4, g1_recv.at[t])
 
-        def body(v, carry):
-            h, d = v % 2, v // 2
-            copy_g1f(t, h, d).start()
-            for side_d in range(2):
-                copy_g2(t, h, side_d, 3 - 2 * d).start()
-            return carry
-
-        lax.fori_loop(0, 4, body, 0)
+        for h in range(2):
+            for d in range(2):
+                copy_g1f(t, h, d).start()
+        for d in range(2):
+            for h in range(2):
+                for side_d in range(2):
+                    copy_g2(t, h, side_d, 3 - 2 * d).start()
 
     def gather_2(t):
         wait_all(abuf, 2, g1f_recv.at[t])
@@ -611,10 +611,10 @@
         ([(misfit_parts,), (gather_1, 0)], (0, 0), (0, 0), (1, 2)),
         ([(gather_1, 1)], (1, 0), (0, 0), (1, 2)),
         ([(gather_lane, 0, 0), (misfit_sums,)], (0, 0), (1, 2), (0, 0)),
-        ([(gather_lane, 1, 0)], (1, 0), (1, 2), (0, 0)),
-        ([(gather_lane, 0, 1)], (0, 0), (1, 2), (1, 0)),
-        ([(gather_2, 0), (gather_lane, 0, 3)], (0, 0), (1, 2), (3, 0)),
-        ([(gather_2, 1)], (0, 1), (0, 0), (2, 0)),
+        ([(gather_2, 0), (gather_lane, 1, 0)], (1, 0), (1, 2), (0, 0)),
+        ([(gather_2, 1), (gather_lane, 0, 1)], (0, 0), (1, 2), (1, 0)),
+        ([(gather_lane, 0, 3)], (0, 0), (1, 2), (3, 0)),
+        ([], (0, 1), (0, 0), (2, 0)),
         ([(gather_lane, 1, 1)], (1, 0), (1, 2), (1, 0)),
         ([(gather_lane, 1, 3)], (1, 0), (1, 2), (3, 0)),
         ([(gather_end, 0)], (0, 1), (2, 0), (0, 0)),

time: 61.2 us -> 60.7 us (level)
  no operation moved by 1% of the time
where the time goes in v8:
time: 60.7 us; the launch traced here: 60.5 us
  Pallas kernels  59.9 us (99%)
  between operations  0.64 us (1%)
    pallas_call x1, Pallas kernels, local(): pl.pallas_call(functools.partial(kernel, freq_devices), out_shape=(jax.Sh...  58.6 us
    pallas_call x1, Pallas kernels, local(): pl.pallas_call(hand_on, out_shape=(jax.ShapeDtypeStruct(gradient.shape, f...  1.26 us

profile of v8, /device:TPU:1, one launch (start us, length us, event | category | flops | bytes accessed | tf_op | source)
XLA Modules:
  0.0 60.5 jit_solution(6295611390925374760)
XLA Ops:
  0.6 58.6 %misfit_gradient.1 = (f32[2,256]{1,0:T(2,128)}, f32[2,32]{1,0:T(2,128)}) custom-call(s32[1,64]{1,0:T(1,128)} %bitcast.5, s32[2,64]{1,0:T(2,128)} %bitcast.4, f32[2,256]{1,0:T(2,128)} %psd_hbm.1, bf16[8,96,128]{2,1,0:T(8,128)(2,1)} %constant.2.clone.table, bf16[2,2,16,128,256]{4,3,2,1,0:T(8,128)(2,1)} %bitcast.3, bf16[2,128,128,128]{3,2,1,0:T(8,128)(2,1)} %observed.1), custom_call_target="tpu_custom_call" | custom-call | flops 8589934592 | bytes 12582912 | tf_op jit(solution)/shard_map/misfit_gradient/pallas_call | solution.py:698
  59.3 1.3 %hand_on.1 = (f32[2,256]{1,0:T(2,128)}, f32[2,32]{1,0:T(2,128)}) custom-call(f32[2,256]{1,0:T(2,128)} %get-tuple-element.4.gradient, f32[2,32]{1,0:T(2,128)} %get-tuple-element.5.misfit), custom_call_target="tpu_custom_call" | custom-call | tf_op jit(solution)/shard_map/hand_on/pallas_call | solution.py:781

commit v9 on v8

--- a/solution.py
+++ b/solution.py
@@ -610,11 +610,11 @@
         ([], (0, 1), (0, 0), (0, 0)),
         ([(misfit_parts,), (gather_1, 0)], (0, 0), (0, 0), (1, 2)),
         ([(gather_1, 1)], (1, 0), (0, 0), (1, 2)),
-        ([(gather_lane, 0, 0), (misfit_sums,)], (0, 0), (1, 2), (0, 0)),
+        ([(gather_lane, 0, 0)], (0, 0), (1, 2), (0, 0)),
         ([(gather_2, 0), (gather_lane, 1, 0)], (1, 0), (1, 2), (0, 0)),
         ([(gather_2, 1), (gather_lane, 0, 1)], (0, 0), (1, 2), (1, 0)),
         ([(gather_lane, 0, 3)], (0, 0), (1, 2), (3, 0)),
-        ([], (0, 1), (0, 0), (2, 0)),
+        ([(misfit_sums,)], (0, 1), (0, 0), (2, 0)),
         ([(gather_lane, 1, 1)], (1, 0), (1, 2), (1, 0)),
         ([(gather_lane, 1, 3)], (1, 0), (1, 2), (3, 0)),
         ([(gather_end, 0)], (0, 1), (2, 0), (0, 0)),
@@ -676,9 +676,15 @@
     wait_all(abuf, 30 * stages, g_send.at[0])
 
 
-def hand_on(gradient, misfit, gradient_out, misfit_out):
-    gradient_out[...] = gradient[...]
-    misfit_out[...] = misfit[...]
+def hand_on(gradient, misfit, gradient_out, misfit_out, sems):
+    copies = [
+        pltpu.make_async_copy(gradient, gradient_out, sems.at[0]),
+        pltpu.make_async_copy(misfit, misfit_out, sems.at[1]),
+    ]
+    for copy in copies:
+        copy.start()
+    for copy in copies:
+        copy.wait()
 
 
 def local(green_spectra, source_psd, pair_list, owner_map, observed):
@@ -784,8 +790,9 @@
             jax.ShapeDtypeStruct(gradient.shape, f32),
             jax.ShapeDtypeStruct(misfit.shape, f32),
         ),
-        in_specs=[vmem, vmem],
-        out_specs=(vmem, vmem),
+        in_specs=[hbm, hbm],
+        out_specs=(hbm, hbm),
+        scratch_shapes=[dma((2,))],
         name="hand_on",
     )(gradient, misfit)
 

time: 60.7 us -> 60.6 us (level)
  no operation moved by 1% of the time
where the time goes in v9:
time: 60.6 us; the launch traced here: 60.5 us
  Pallas kernels  59.9 us (99%)
  between operations  0.64 us (1%)
    pallas_call x1, Pallas kernels, local(): pl.pallas_call(functools.partial(kernel, freq_devices), out_shape=(jax.Sh...  58.6 us
    pallas_call x1, Pallas kernels, local(): pl.pallas_call(hand_on, out_shape=(jax.ShapeDtypeStruct(gradient.shape, f...  1.21 us

profile of v9, /device:TPU:1, one launch (start us, length us, event | category | flops | bytes accessed | tf_op | source)
XLA Modules:
  0.0 60.5 jit_solution(11935595867380420903)
XLA Ops:
  0.6 58.6 %misfit_gradient.1 = (f32[2,256]{1,0:T(2,128)}, f32[2,32]{1,0:T(2,128)}) custom-call(s32[1,64]{1,0:T(1,128)} %bitcast.5, s32[2,64]{1,0:T(2,128)} %bitcast.4, f32[2,256]{1,0:T(2,128)} %psd_hbm.1, bf16[8,96,128]{2,1,0:T(8,128)(2,1)} %constant.2.clone.table, bf16[2,2,16,128,256]{4,3,2,1,0:T(8,128)(2,1)} %bitcast.3, bf16[2,128,128,128]{3,2,1,0:T(8,128)(2,1)} %observed.1), custom_call_target="tpu_custom_call" | custom-call | flops 8589934592 | bytes 12582912 | tf_op jit(solution)/shard_map/misfit_gradient/pallas_call | solution.py:704
  59.3 1.2 %hand_on.1 = (f32[2,256]{1,0:T(2,128)}, f32[2,32]{1,0:T(2,128)}) custom-call(f32[2,256]{1,0:T(2,128)} %get-tuple-element.4.gradient, f32[2,32]{1,0:T(2,128)} %get-tuple-element.5.misfit), custom_call_target="tpu_custom_call" | custom-call | tf_op jit(solution)/shard_map/hand_on/pallas_call | solution.py:787
